TPU v7x, 128 devices: a whole 4x4x4 slice. The times are simulated.
128 devices in a mesh: dp: 2 (over core), row: 4 (over x), col: 16 (over y, z).
Axes of the slice: x: 4, y: 4, z: 4, core: 2. Of those that a mesh axis runs over, the one named last changes fastest.
Arguments:
- tokens: bfloat16 [18912, 1024], P(('dp', 'col'), 'row'), may hold values from -6 to 6
- norm_gain: float32 [2, 2, 1024], P(None, None, 'row'), may hold values from 0.5 to 1.5
- norm_shift: float32 [2, 2, 1024], P(None, None, 'row'), may hold values from -3 to 3
- qkv_weight: bfloat16 [2, 1024, 3072], P(None, 'row', 'col')
- qv_bias: float32 [2, 2048], P(None, 'col'), may hold values from -3 to 3
- proj_weight: bfloat16 [2, 1024, 1024], P(None, 'col', 'row'), may hold values from -0.75 to 0.75
- proj_bias: float32 [2, 1024], P(None, 'row'), may hold values from -3 to 3
- up_weight: bfloat16 [2, 1024, 4096], P(None, 'row', 'col'), may hold values from -0.1875 to 0.1875
- up_bias: float32 [2, 4096], P(None, 'col'), may hold values from -3 to 3
- down_weight: bfloat16 [2, 4096, 1024], P(None, 'col', 'row'), may hold values from -0.09375 to 0.09375
- down_bias: float32 [2, 1024], P(None, 'row'), may hold values from -3 to 3
- cotangent: float32 [18912, 1024], P(('dp', 'col'), 'row'), may hold values from -6 to 6
Outputs:
- encoded: float32 [18912, 1024], P(('dp', 'col'), 'row')
- grad_tokens: float32 [18912, 1024], P(('dp', 'col'), 'row')
- grad_norm_gain: float32 [2, 2, 1024], P(None, None, 'row')
- grad_norm_shift: float32 [2, 2, 1024], P(None, None, 'row')
- grad_qkv_weight: float32 [2, 1024, 3072], P(None, 'row', 'col')
- grad_qv_bias: float32 [2, 2048], P(None, 'col')
- grad_proj_weight: float32 [2, 1024, 1024], P(None, 'col', 'row')
- grad_proj_bias: float32 [2, 1024], P(None, 'row')
- grad_up_weight: float32 [2, 1024, 4096], P(None, 'row', 'col')
- grad_up_bias: float32 [2, 4096], P(None, 'col')
- grad_down_weight: float32 [2, 4096, 1024], P(None, 'col', 'row')
- grad_down_bias: float32 [2, 1024], P(None, 'row')
All inputs are finite; a program needn't handle non-finite values.
Results may differ from a plain program's by a relative error of at most 0.03.
Values may be sent and summed in bfloat16 or wider, within the bound.
A program may use at most 256 MiB of HBM per device.

v0:
```python
from functools import partial

import jax
import jax.numpy as jnp
from jax import lax
from jax.sharding import PartitionSpec as P

HEAD = 64
SEQ = 197


def contract(left_rows, matrix, inner):
    return lax.dot_general(
        left_rows, matrix, (((1,), (inner,)), ((), ())), preferred_element_type=jnp.float32
    )


def outer_sum(left_rows, right_rows):
    return lax.dot_general(
        left_rows, right_rows, (((0,), (0,)), ((), ())), preferred_element_type=jnp.float32
    )


def col_then_row(local, matrix, inner):
    gathered = lax.all_gather(local, "col", axis=0, tiled=True)
    return (
        gathered,
        lax.psum_scatter(
            contract(gathered, matrix, inner).astype(jnp.bfloat16),
            "row",
            scatter_dimension=0,
            tiled=True,
        ).astype(jnp.float32),
    )


def row_then_col(local, matrix, inner):
    gathered = lax.all_gather(local, "row", axis=0, tiled=True)
    return (
        gathered,
        lax.psum_scatter(
            contract(gathered, matrix, inner).astype(jnp.bfloat16),
            "col",
            scatter_dimension=0,
            tiled=True,
        ).astype(jnp.float32),
    )


def again_cols(kept):
    return lax.all_gather(kept, "col", axis=0, tiled=True)


def again_rows(kept):
    return lax.all_gather(kept, "row", axis=0, tiled=True)


def normalize(resid, gain, shift):
    width = resid.shape[1] * lax.axis_size("row")
    average = lax.psum(jnp.sum(resid, axis=1), "row") / width
    centered = resid - average[:, None]
    variance = lax.psum(jnp.sum(centered * centered, axis=1), "row") / width
    inv_spread = lax.rsqrt(variance + 1e-06)[:, None]
    normed = centered * inv_spread
    return (normed * gain + shift, normed, inv_spread)


def normalize_back(incoming, normed, inv_spread, gain):
    width = incoming.shape[1] * lax.axis_size("row")
    scaled = incoming * gain
    totals, along = lax.psum((jnp.sum(scaled, axis=1), jnp.sum(scaled * normed, axis=1)), "row")
    result = inv_spread * (scaled - totals[:, None] / width - normed * along[:, None] / width)
    return (result, jnp.sum(incoming * normed, axis=0), jnp.sum(incoming, axis=0))


def split_heads(mixed):
    images = mixed.shape[0] // SEQ
    split = mixed.reshape(images, SEQ, -1, 3, HEAD)
    return (split[:, :, :, 0], split[:, :, :, 1], split[:, :, :, 2])


def scores_of(queries, keys_in):
    raw_scores = jnp.einsum("gqhe,gkhe->ghqk", queries, keys_in, preferred_element_type=jnp.float32)
    return raw_scores * HEAD ** (-0.5)


def attend_forward(mixed):
    queries, keys_in, values_in = split_heads(mixed)
    scores = scores_of(queries, keys_in)
    highest = jnp.max(scores, axis=-1, keepdims=True)
    expon = jnp.exp(scores - highest)
    summed = jnp.sum(expon, axis=-1, keepdims=True)
    softmax_low = (expon / summed).astype(jnp.bfloat16)
    attended = jnp.einsum(
        "ghqk,gkhe->gqhe", softmax_low, values_in, preferred_element_type=jnp.float32
    )
    return (attended.reshape(mixed.shape[0], -1).astype(jnp.bfloat16), highest + jnp.log(summed))


def attend_backward(mixed, log_total, grad_out):
    queries, keys_in, values_in = split_heads(mixed)
    scores = scores_of(queries, keys_in)
    softmax_w = jnp.exp(scores - log_total)
    softmax_low = softmax_w.astype(jnp.bfloat16)
    grad_split = grad_out.reshape(queries.shape)
    grad_weights = jnp.einsum(
        "gqhe,gkhe->ghqk", grad_split, values_in, preferred_element_type=jnp.float32
    )
    grad_values = jnp.einsum(
        "ghqk,gqhe->gkhe", softmax_low, grad_split, preferred_element_type=jnp.float32
    )
    centre = jnp.sum(softmax_w * grad_weights, axis=-1, keepdims=True)
    grad_scores = (softmax_w * (grad_weights - centre) * HEAD ** (-0.5)).astype(jnp.bfloat16)
    grad_queries = jnp.einsum(
        "ghqk,gkhe->gqhe", grad_scores, keys_in, preferred_element_type=jnp.float32
    )
    grad_keys = jnp.einsum(
        "ghqk,gqhe->gkhe", grad_scores, queries, preferred_element_type=jnp.float32
    )
    stacked = jnp.stack([grad_queries, grad_keys, grad_values], axis=3).astype(jnp.bfloat16)
    return stacked.reshape(mixed.shape)


def shards(
    tokens,
    norm_gain,
    norm_shift,
    qkv_weight,
    qv_bias,
    proj_weight,
    proj_bias,
    up_weight,
    up_bias,
    down_weight,
    down_bias,
    cotangent,
):
    resid = tokens.astype(jnp.float32)
    layers = qkv_weight.shape[0]
    saved = []
    for layer_no in range(layers):
        normed_out, normed_in, spread_in = normalize(
            resid, norm_gain[layer_no, 0], norm_shift[layer_no, 0]
        )
        normed_low = normed_out.astype(jnp.bfloat16)
        gathered_in, mixed = col_then_row(normed_low, qkv_weight[layer_no], 0)
        paired = qv_bias[layer_no].reshape(-1, 2, HEAD)
        bias_full = jnp.concatenate(
            [paired[:, 0:1], jnp.zeros_like(paired[:, 0:1]), paired[:, 1:2]], axis=1
        ).reshape(-1)
        mixed = (mixed + bias_full).astype(jnp.bfloat16)
        attended, log_total = attend_forward(mixed)
        gathered_att, branch = row_then_col(attended, proj_weight[layer_no], 0)
        middle = resid + (branch + proj_bias[layer_no])
        mid_out, normed_mid, spread_mid = normalize(
            middle, norm_gain[layer_no, 1], norm_shift[layer_no, 1]
        )
        mid_low = mid_out.astype(jnp.bfloat16)
        gathered_mid, upward = col_then_row(mid_low, up_weight[layer_no], 0)
        upward = upward + up_bias[layer_no]
        activated = jax.nn.gelu(upward, approximate=False).astype(jnp.bfloat16)
        gathered_act, downward = row_then_col(activated, down_weight[layer_no], 0)
        saved.append(
            (
                normed_low,
                normed_in,
                spread_in,
                mixed,
                log_total,
                attended,
                normed_mid,
                spread_mid,
                mid_low,
                upward,
                activated,
            )
        )
        resid = middle + (downward + down_bias[layer_no])
    incoming = cotangent
    results = [None] * layers
    for layer_no in reversed(range(layers)):
        (
            kept_in,
            normed_in,
            spread_in,
            mixed,
            log_total,
            kept_att,
            normed_mid,
            spread_mid,
            kept_mid,
            upward,
            kept_act,
        ) = saved[layer_no]
        grad_low = incoming.astype(jnp.bfloat16)
        down_gathered, grad_act = col_then_row(grad_low, down_weight[layer_no], 1)
        grad_down = outer_sum(again_rows(kept_act), down_gathered)
        grad_down_bias = jnp.sum(down_gathered, axis=0, dtype=jnp.float32)
        _, gelu_pull = jax.vjp(partial(jax.nn.gelu, approximate=False), upward)
        grad_up_low = gelu_pull(grad_act)[0].astype(jnp.bfloat16)
        up_gathered, grad_hmid = row_then_col(grad_up_low, up_weight[layer_no], 1)
        grad_up = outer_sum(again_cols(kept_mid), up_gathered)
        grad_up_bias = jnp.sum(up_gathered, axis=0, dtype=jnp.float32)
        part_mid, gain_mid, shift_mid = normalize_back(
            grad_hmid, normed_mid, spread_mid, norm_gain[layer_no, 1]
        )
        grad_middle = incoming + part_mid
        att_low = grad_middle.astype(jnp.bfloat16)
        att_gathered, grad_attended = col_then_row(att_low, proj_weight[layer_no], 1)
        grad_proj = outer_sum(again_rows(kept_att), att_gathered)
        grad_proj_bias = jnp.sum(att_gathered, axis=0, dtype=jnp.float32)
        grad_mixed = attend_backward(mixed, log_total, grad_attended.astype(jnp.bfloat16))
        mixed_gathered, grad_hin = row_then_col(grad_mixed, qkv_weight[layer_no], 1)
        grad_qkv = outer_sum(again_cols(kept_in), mixed_gathered)
        bias_sums = jnp.sum(mixed_gathered, axis=0, dtype=jnp.float32).reshape(-1, 3, HEAD)
        grad_qv = jnp.concatenate([bias_sums[:, 0:1], bias_sums[:, 2:3]], axis=1).reshape(-1)
        part_in, gain_in, shift_in = normalize_back(
            grad_hin, normed_in, spread_in, norm_gain[layer_no, 0]
        )
        incoming = grad_middle + part_in
        weight_sums = (
            lax.psum(grad_qkv.astype(jnp.bfloat16), "dp").astype(jnp.float32),
            lax.psum(grad_qv.astype(jnp.bfloat16), "dp").astype(jnp.float32),
            lax.psum(grad_proj.astype(jnp.bfloat16), "dp").astype(jnp.float32),
            lax.psum(grad_proj_bias.astype(jnp.bfloat16), "dp").astype(jnp.float32),
            lax.psum(grad_up.astype(jnp.bfloat16), "dp").astype(jnp.float32),
            lax.psum(grad_up_bias.astype(jnp.bfloat16), "dp").astype(jnp.float32),
            lax.psum(grad_down.astype(jnp.bfloat16), "dp").astype(jnp.float32),
            lax.psum(grad_down_bias.astype(jnp.bfloat16), "dp").astype(jnp.float32),
        )
        norm_sums = lax.psum(
            (jnp.stack([gain_in, gain_mid]), jnp.stack([shift_in, shift_mid])), ("dp", "col")
        )
        results[layer_no] = tuple(weight_sums) + tuple(norm_sums)
    stacked = [
        jnp.stack([results[index][member] for index in range(layers)]) for member in range(10)
    ]
    return (
        resid,
        incoming,
        stacked[8],
        stacked[9],
        stacked[0],
        stacked[1],
        stacked[2],
        stacked[3],
        stacked[4],
        stacked[5],
        stacked[6],
        stacked[7],
    )


def solution(mesh):
    in_specs = (
        P(("dp", "col"), "row"),
        P(None, None, "row"),
        P(None, None, "row"),
        P(None, "row", "col"),
        P(None, "col"),
        P(None, "col", "row"),
        P(None, "row"),
        P(None, "row", "col"),
        P(None, "col"),
        P(None, "col", "row"),
        P(None, "row"),
        P(("dp", "col"), "row"),
    )
    out_specs = (
        P(("dp", "col"), "row"),
        P(("dp", "col"), "row"),
        P(None, None, "row"),
        P(None, None, "row"),
        P(None, "row", "col"),
        P(None, "col"),
        P(None, "col", "row"),
        P(None, "row"),
        P(None, "row", "col"),
        P(None, "col"),
        P(None, "col", "row"),
        P(None, "row"),
    )
    return jax.shard_map(shards, mesh=mesh, in_specs=in_specs, out_specs=out_specs, check_vma=False)
```

profile of v0, /device:TPU:1, one launch (start us, length us, event | category | flops | bytes accessed | tf_op | source)
XLA Modules:
  0.0 2347.9 jit_solution(9258418994528750272)
XLA Ops:
  29.0 59.9 %all-gather.33.cloned.1.call-done = bf16[16,591,256]{2,1,0:T(8,128)(2,1)} async-done(((bf16[1,591,256]{2,1,0:T(8,128)(2,1)}), bf16[16,591,256]{2,1,0:T(8,128)(2,1)}) %all-gather.33.cloned.1.call-update) | async-done | bytes 4841488 | tf_op jit(solution)/shard_map/all_gather | solution.py:25
  101.9 81.1 %all-reduce.44.cloned.1.call-done = bf16[9456,192]{0,1:T(8,128)(2,1)} async-done(((bf16[9456,192]{0,1:T(8,128)(2,1)}), bf16[9456,192]{0,1:T(8,128)(2,1)}) %all-reduce.44.cloned.1.call-update) | async-done | bytes 3631120
  226.7 64.3 %fusion = bf16[592,256]{1,0:T(8,128)(2,1)S(1)} fusion(bf16[9456,256]{1,0:T(8,128)(2,1)} %convolution_convert_fusion.9), kind=kCustom, calls=%all-reduce-scatter | all-reduce-scatter fusion | flops 2424833 | bytes 5145088
  311.2 60.8 %all-gather.37.cloned.1.call-done = bf16[16,591,256]{2,1,0:T(8,128)(2,1)} async-done(((bf16[1,591,256]{2,1,0:T(8,128)(2,1)}), bf16[16,591,256]{2,1,0:T(8,128)(2,1)}) %all-gather.37.cloned.1.call-update) | async-done | bytes 4841488 | tf_op jit(solution)/shard_map/all_gather | solution.py:25
  382.6 60.9 %fusion.1 = bf16[2368,256]{1,0:T(8,128)(2,1)} fusion(bf16[9456,256]{1,0:T(8,128)(2,1)} %convolution_convert_fusion.7), kind=kCustom, calls=%all-reduce-scatter.1 | all-reduce-scatter fusion | flops 2424833 | bytes 6054400
  461.2 55.8 %all-gather.39.cloned.1.call-done = bf16[4,2364,256]{2,1,0:T(8,128)(2,1)} async-done(((bf16[1,2364,256]{2,1,0:T(8,128)(2,1)}), bf16[4,2364,256]{2,1,0:T(8,128)(2,1)}) %all-gather.39.cloned.1.call-update) | async-done | bytes 4841488 | tf_op jit(solution)/shard_map/all_gather | solution.py:38
  527.5 62.9 %fusion.2 = bf16[592,256]{1,0:T(8,128)(2,1)S(1)} fusion(bf16[9456,256]{1,0:T(8,128)(2,1)} %convolution_convert_fusion.6), kind=kCustom, calls=%all-reduce-scatter.2 | all-reduce-scatter fusion | flops 2424833 | bytes 5145088
  613.1 61.9 %all-gather.41.cloned.1.call-done = bf16[16,591,256]{2,1,0:T(8,128)(2,1)} async-done(((bf16[1,591,256]{2,1,0:T(8,128)(2,1)}), bf16[16,591,256]{2,1,0:T(8,128)(2,1)}) %all-gather.41.cloned.1.call-update) | async-done | bytes 4841488 | tf_op jit(solution)/shard_map/all_gather | solution.py:25
  685.7 83.3 %all-reduce.46.cloned.1.call-done = bf16[9456,192]{0,1:T(8,128)(2,1)} async-done(((bf16[9456,192]{0,1:T(8,128)(2,1)}), bf16[9456,192]{0,1:T(8,128)(2,1)}) %all-reduce.46.cloned.1.call-update) | async-done | bytes 3631120
  818.7 82.9 %fusion.3 = bf16[592,256]{1,0:T(8,128)(2,1)S(1)} fusion(bf16[9456,256]{1,0:T(8,128)(2,1)} %convolution_convert_fusion.8), kind=kCustom, calls=%all-reduce-scatter.3 | all-reduce-scatter fusion | flops 2424833 | bytes 5145088
  936.3 51.0 %all-gather.45.cloned.1.call-done = bf16[16,591,256]{2,1,0:T(8,128)(2,1)} async-done(((bf16[1,591,256]{2,1,0:T(8,128)(2,1)}), bf16[16,591,256]{2,1,0:T(8,128)(2,1)}) %all-gather.45.cloned.1.call-update) | async-done | bytes 4841488 | tf_op jit(solution)/shard_map/all_gather | solution.py:25
  997.8 112.3 %fusion.224 = (bf16[2368,256]{1,0:T(8,128)(2,1)}, bf16[2368,256]{1,0:T(8,128)(2,1)}) fusion(bf16[9456,256]{1,0:T(8,128)(2,1)} %convolution_convert_fusion.5, bf16[9456,256]{1,0:T(8,128)(2,1)} %convolution_convert_fusion.3), kind=kCustom, calls=%all-reduce-scatter.13 | all-reduce-scatter fusion | flops 4849665 | bytes 12108288
  1140.4 53.0 %all-gather.51.cloned.1.call-done = bf16[4,2364,256]{2,1,0:T(8,128)(2,1)} async-done(((bf16[1,2364,256]{2,1,0:T(8,128)(2,1)}), bf16[4,2364,256]{2,1,0:T(8,128)(2,1)}) %all-gather.51.cloned.1.call-update) | async-done | bytes 4841488 | tf_op jit(solution)/shard_map/all_gather | solution.py:38
  1203.8 63.5 %fusion.7 = bf16[592,256]{1,0:T(8,128)(2,1)} fusion(bf16[9456,256]{1,0:T(8,128)(2,1)} %convolution_convert_fusion.2), kind=kCustom, calls=%all-reduce-scatter.7 | all-reduce-scatter fusion | flops 2424833 | bytes 5145088
  1288.1 59.0 %all-gather.53.cloned.1.call-done = bf16[16,591,256]{2,1,0:T(8,128)(2,1)} async-done(((bf16[1,591,256]{2,1,0:T(8,128)(2,1)}), bf16[16,591,256]{2,1,0:T(8,128)(2,1)}) %all-gather.53.cloned.1.call-update) | async-done | bytes 4841488 | tf_op jit(solution)/shard_map/all_gather | solution.py:25
  1430.1 46.4 %all-gather.55.cloned.1.call-done = bf16[4,2364,192]{1,2,0:T(8,128)(2,1)} async-done(((bf16[1,2364,192]{1,2,0:T(8,128)(2,1)}), bf16[4,2364,192]{1,2,0:T(8,128)(2,1)}) %all-gather.55.cloned.1.call-update) | async-done | bytes 3631120 | tf_op jit(solution)/shard_map/all_gather | solution.py:38
  1495.8 63.3 %fusion.8 = bf16[592,256]{1,0:T(8,128)(2,1)} fusion(bf16[9456,256]{1,0:T(8,128)(2,1)} %convolution_convert_fusion.11), kind=kCustom, calls=%all-reduce-scatter.8 | all-reduce-scatter fusion | flops 2424833 | bytes 5145088
  1578.2 59.0 %all-gather.57.cloned.1.call-done = bf16[16,591,256]{2,1,0:T(8,128)(2,1)} async-done(((bf16[1,591,256]{2,1,0:T(8,128)(2,1)}), bf16[16,591,256]{2,1,0:T(8,128)(2,1)}) %all-gather.57.cloned.1.call-update) | async-done | bytes 4841488 | tf_op jit(solution)/shard_map/all_gather | solution.py:25
  1647.9 60.8 %fusion.9 = bf16[2368,256]{1,0:T(8,128)(2,1)} fusion(bf16[9456,256]{1,0:T(8,128)(2,1)} %convolution_convert_fusion.1), kind=kCustom, calls=%all-reduce-scatter.9 | all-reduce-scatter fusion | flops 2424833 | bytes 6054400
  1723.7 55.8 %all-gather.59.cloned.1.call-done = bf16[4,2364,256]{2,1,0:T(8,128)(2,1)} async-done(((bf16[1,2364,256]{2,1,0:T(8,128)(2,1)}), bf16[4,2364,256]{2,1,0:T(8,128)(2,1)}) %all-gather.59.cloned.1.call-update) | async-done | bytes 4841488 | tf_op jit(solution)/shard_map/all_gather | solution.py:38
  1790.1 62.9 %fusion.10 = bf16[592,256]{1,0:T(8,128)(2,1)S(1)} fusion(bf16[9456,256]{1,0:T(8,128)(2,1)} %convolution_convert_fusion), kind=kCustom, calls=%all-reduce-scatter.10 | all-reduce-scatter fusion | flops 2424833 | bytes 5145088
  1869.1 59.0 %all-gather.61.cloned.1.call-done = bf16[16,591,256]{2,1,0:T(8,128)(2,1)} async-done(((bf16[1,591,256]{2,1,0:T(8,128)(2,1)}), bf16[16,591,256]{2,1,0:T(8,128)(2,1)}) %all-gather.61.cloned.1.call-update) | async-done | bytes 4841488 | tf_op jit(solution)/shard_map/all_gather | solution.py:25
  2127.5 112.1 %fusion.223 = (bf16[592,256]{1,0:T(8,128)(2,1)S(1)}, bf16[592,256]{1,0:T(8,128)(2,1)S(1)}) fusion(bf16[9456,256]{1,0:T(8,128)(2,1)} %convolution_convert_fusion.4, bf16[9456,256]{1,0:T(8,128)(2,1)} %convolution_convert_fusion.10), kind=kCustom, calls=%all-reduce-scatter.12 | all-reduce-scatter fusion | flops 4849665 | bytes 10289664
  2260.6 67.2 %all-reduce.28 = (f32[1,2,256]{2,1,0:T(2,128)S(1)}, f32[1,2,256]{2,1,0:T(2,128)S(1)}, f32[1,2,256]{2,1,0:T(2,128)S(1)}, f32[1,2,256]{2,1,0:T(2,128)S(1)}) all-reduce(f32[1,2,256]{2,1,0:T(2,128)S(1)} %maximum_bitcast_fusion.1, f32[1,2,256]{2,1,0:T(2,128)S(1)} %maximum_bitcast_fusion, ...), channel_id=1, replica_groups=mesh['dp'=2,'row'=4,'col'=16] {'dp','col'}, use_global_device_ids=true, to_apply=%region_59.0 | all-reduce | flops 2048 | bytes 16384 | tf_op jit(solution)/shard_map/psum | solution.py:231
  (395 shorter events, 730.7 us)
Async XLA Ops:
  7.2 81.8 %all-gather.33.cloned.1.call-start = ((), (), s32[]{:S(2)}) async-start(), calls=%async_computation | async-start | bytes 5152768 | tf_op jit(solution)/shard_map/all_gather | solution.py:25
  29.0 154.0 %all-reduce.44.cloned.1.call-start = ((), (), s32[]{:S(2)}) async-start(), calls=%async_computation.16 | async-start | bytes 7274496
  99.6 115.9 %all-gather.35.cloned.1.call-start = ((), (), s32[]{:S(2)}) async-start(), calls=%async_computation.1 | async-start | bytes 1556480 | tf_op jit(solution)/shard_map/all_gather | solution.py:38
  191.9 180.1 %all-gather.37.cloned.1.call-start = ((), (), s32[]{:S(2)}) async-start(), calls=%async_computation.2 | async-start | bytes 5152768 | tf_op jit(solution)/shard_map/all_gather | solution.py:25
  311.2 205.9 %all-gather.39.cloned.1.call-start = ((), (), s32[]{:S(2)}) async-start(), calls=%async_computation.3 | async-start | bytes 6062080 | tf_op jit(solution)/shard_map/all_gather | solution.py:38
  461.2 213.8 %all-gather.41.cloned.1.call-start = ((), (), s32[]{:S(2)}) async-start(), calls=%async_computation.4 | async-start | bytes 5152768 | tf_op jit(solution)/shard_map/all_gather | solution.py:25
  613.0 155.9 %all-reduce.46.cloned.1.call-start = ((), (), s32[]{:S(2)}) async-start(), calls=%async_computation.17 | async-start | bytes 7274496
  685.5 121.9 %all-gather.43.cloned.1.call-start = ((), (), s32[]{:S(2)}) async-start(), calls=%async_computation.5 | async-start | bytes 1556480 | tf_op jit(solution)/shard_map/all_gather | solution.py:38
  783.8 141.8 %all-gather.49.cloned.1.call-start = ((), (), s32[]{:S(2)}) async-start(), calls=%async_computation.8 | async-start | bytes 5152768 | tf_op jit(solution)/shard_map/all_gather | solution.py:25
  784.7 202.6 %all-gather.45.cloned.1.call-start = ((), (), s32[]{:S(2)}) async-start(), calls=%async_computation.6 | async-start | bytes 5152768 | tf_op jit(solution)/shard_map/all_gather | solution.py:25
  925.6 267.8 %all-gather.51.cloned.1.call-start = ((), (), s32[]{:S(2)}) async-start(), calls=%async_computation.9 | async-start | bytes 6062080 | tf_op jit(solution)/shard_map/all_gather | solution.py:38
  1140.3 206.8 %all-gather.53.cloned.1.call-start = ((), (), s32[]{:S(2)}) async-start(), calls=%async_computation.10 | async-start | bytes 5152768 | tf_op jit(solution)/shard_map/all_gather | solution.py:25
  1288.0 114.0 %all-reduce.48.cloned.1.call-start = ((), (), s32[]{:S(2)}) async-start(), calls=%async_computation.18 | async-start | bytes 2424832
  1356.8 119.7 %all-gather.55.cloned.1.call-start = ((), (), s32[]{:S(2)}) async-start(), calls=%async_computation.11 | async-start | bytes 4669440 | tf_op jit(solution)/shard_map/all_gather | solution.py:38
  1429.8 207.4 %all-gather.57.cloned.1.call-start = ((), (), s32[]{:S(2)}) async-start(), calls=%async_computation.12 | async-start | bytes 5152768 | tf_op jit(solution)/shard_map/all_gather | solution.py:25
  1578.1 201.4 %all-gather.59.cloned.1.call-start = ((), (), s32[]{:S(2)}) async-start(), calls=%async_computation.13 | async-start | bytes 6062080 | tf_op jit(solution)/shard_map/all_gather | solution.py:38
  1723.7 204.5 %all-gather.61.cloned.1.call-start = ((), (), s32[]{:S(2)}) async-start(), calls=%async_computation.14 | async-start | bytes 5152768 | tf_op jit(solution)/shard_map/all_gather | solution.py:25
  1869.1 114.0 %all-reduce.50.cloned.1.call-start = ((), (), s32[]{:S(2)}) async-start(), calls=%async_computation.19 | async-start | bytes 2424832
  1937.9 102.7 %all-gather.47.cloned.1.call-start = ((), (), s32[]{:S(2)}) async-start(), calls=%async_computation.7 | async-start | bytes 6062080 | tf_op jit(solution)/shard_map/all_gather | solution.py:38
  1941.5 163.2 %all-gather.63.cloned.1.call-start = ((), (), s32[]{:S(2)}) async-start(), calls=%async_computation.15 | async-start | bytes 4669440 | tf_op jit(solution)/shard_map/all_gather | solution.py:38
  2004.8 324.2 %all-reduce.52.cloned.1.call-start = ((), (), s32[]{:S(2)}) async-start(), calls=%async_computation.20 | async-start | bytes 145408 | tf_op jit(solution)/shard_map/psum | solution.py:223
  2239.6 10.3 collective-permute-start.11
  2242.6 92.8 %all-reduce.54.cloned.1.call-start = ((), (), s32[]{:S(2)}) async-start(), calls=%async_computation.21 | async-start | bytes 1441792 | tf_op jit(solution)/shard_map/psum | solution.py:222
  2247.9 10.0 collective-permute-start.5
  (65 other events, 1707.3 us)
Sparse Core Ops, SparseCore 0:
  29.1 59.8 all-gather.32
  99.7 83.2 all-reduce.43
  192.0 23.4 all-gather.34
  311.3 60.7 all-gather.36
  461.3 55.7 all-gather.38
  613.1 61.8 all-gather.40
  685.6 83.2 all-reduce.45
  784.0 23.4 all-gather.42
  810.2 73.9 all-gather.48
  925.7 61.5 all-gather.44
  1140.4 52.8 all-gather.50
  1288.2 58.9 all-gather.52
  1356.9 45.0 all-reduce.47
  1429.9 46.5 all-gather.54
  1578.2 58.9 all-gather.56
  1723.8 55.7 all-gather.58
  1869.2 58.9 all-gather.60
  1938.0 45.0 all-reduce.49
  1984.7 55.7 all-gather.46
  2042.1 44.8 all-gather.62
  2242.7 24.1 all-reduce.51
  2270.9 26.4 all-reduce.53
where the time goes:
time: 2360 us; the launch traced here: 2350 us
  waiting for transfers between devices  950 us (40%)
  blocking collectives  905 us (38%)
  local copies, waits for them, and re-layouts  188 us (8%)
  matrix products  162 us (7%)
  other arithmetic  100 us (4%)
  starting transfers between devices  25.8 us (1%)
    unnamed x10, blocking collectives  746 us
    all_gather x8, waiting for transfers between devices, col_then_row(): gathered = lax.all_gather(local, 'col', axis=0, tiled=True)  411 us
    all_gather x8, waiting for transfers between devices, row_then_col(): gathered = lax.all_gather(local, 'row', axis=0, tiled=True)  285 us
    unnamed x38, waiting for transfers between devices  255 us
    unnamed x158, local copies, waits for them, and re-layouts  140 us
    dot_general x16, matrix products, contract(): lax.dot_general(left_rows, matrix, (((1,), (inner,)), ((), ())), preferre...  91.5 us
    psum x1, blocking collectives, shards(): lax.psum((jnp.stack([gain_in, gain_mid]), jnp.stack([shift_in, shift_mid]...  67.2 us
  transfers between devices with their start and end apart: 34, of which 25 were waited for; matrix products, arithmetic and copies ran while one was open for 10% of the time, Pallas kernels for 0%

commit v1 on v0

v1 whole, which is shorter than its diff:
```python
import functools

import jax
import jax.numpy as jnp
from jax import lax
from jax.experimental import pallas as pl
from jax.experimental.pallas import tpu as pltpu
from jax.sharding import PartitionSpec as P

MESH = pl.DeviceIdType.MESH
RING = 4
ORDERS = (("x", "y", "z"), ("y", "z", "x"), ("z", "x", "y"))
CUTS = {128: ((0, 48, 32), (48, 48, 16), (96, 32, 16)), 256: ((0, 80, 48), (80, 80, 32), (160, 96, 48))}


class Place:
    def __init__(self):
        self.core = lax.axis_index("dp")
        block = lax.axis_index("col")
        self.at = {"x": lax.axis_index("row"), "y": block // RING, "z": block % RING}

    def shifted(self, axis, by):
        moved = dict(self.at)
        moved[axis] = (self.at[axis] + by + RING) % RING
        return moved

    def device(self, at, core=None):
        return (self.core if core is None else core, at["x"], at["y"] * RING + at["z"])

    def neighbour(self, axis, by):
        return self.device(self.shifted(axis, by))

    def sibling(self):
        return self.device(self.at, 1 - self.core)

    def greet(self):
        barrier = pltpu.get_barrier_semaphore()
        for axis in "xyz":
            for by in (1, -1):
                pl.semaphore_signal(barrier, inc=1, device_id=self.neighbour(axis, by), device_id_type=MESH)
        pl.semaphore_signal(barrier, inc=1, device_id=self.sibling(), device_id_type=MESH)
        pl.semaphore_wait(barrier, 7)


def region(ref, at, whole, start, count):
    index = tuple(pl.ds(0, RING) if a in whole else at[a] for a in "yzx")
    return ref.at[index + (pl.ds(start, count),)]


def remote(src, dst, send, recv, device):
    return pltpu.make_async_remote_copy(
        src_ref=src, dst_ref=dst, send_sem=send, recv_sem=recv, device_id=device, device_id_type=MESH
    )


class Gather:
    def __init__(self, place, own, full, order, start, count, half, send, recv, share):
        self.place, self.own, self.full, self.order = place, own, full, order
        self.start, self.count, self.half = start, count, half
        self.send, self.recv, self.share = send, recv, share
        self.sent = []
        self.shared = []

    def piece(self, phase, by, start, count):
        at = self.place.shifted(self.order[phase], by)
        return region(self.full, at, self.order[:phase], start, count)

    def pass_on(self, ref, send, recv):
        if self.share:
            copy = remote(ref, ref, send, recv, self.place.sibling())
            copy.start()
            self.shared.append(copy)

    def first(self, phase):
        axis = self.order[phase]
        src = self.own if phase == 0 else self.piece(phase, 0, self.start, self.count)
        dst = self.piece(phase, 0, self.start, self.count)
        self.now = []
        for i, by in enumerate((1, -1)):
            copy = remote(src, dst, self.send.at[phase, i], self.recv.at[phase, i], self.place.neighbour(axis, by))
            copy.start()
            self.now.append(copy)
        self.sent += self.now

    def second(self, phase):
        axis = self.order[phase]
        later = []
        for i, by in enumerate((1, -1)):
            self.now[i].wait_recv()
            start, count = (self.start, self.half) if i == 0 else (self.start + self.half, self.count - self.half)
            ref = self.piece(phase, -by, start, count)
            copy = remote(ref, ref, self.send.at[phase, 2 + i], self.recv.at[phase, 2 + i], self.place.neighbour(axis, by))
            copy.start()
            later.append(copy)
        for i, by in enumerate((1, -1)):
            if self.share:
                self.pass_on(self.piece(phase, -by, self.start, self.count), self.send.at[phase, 4 + i], self.recv.at[phase, 4 + i])
        self.now = later
        self.sent += later

    def third(self, phase):
        for i in range(2):
            self.now[i].wait_recv()
            if self.share:
                start, count = (self.start, self.half) if i == 0 else (self.start + self.half, self.count - self.half)
                self.pass_on(self.piece(phase, 2, start, count), self.send.at[phase, 6 + i], self.recv.at[phase, 6 + i])

    def finish(self):
        for copy in self.sent:
            copy.wait_send()
        for copy in self.shared:
            copy.wait_send()
            copy.wait_recv()


def gather_kernel(units, plan, *refs):
    n = len(units)
    own, small, full, small_full = refs[:n], refs[n], refs[n + 1 : 2 * n + 1], refs[2 * n + 1]
    send, recv, small_send, small_recv, local = refs[2 * n + 2 :]
    place = Place()
    place.greet()
    copies = [
        pltpu.make_async_copy(own[u], region(full[u], place.at, (), 0, units[u]), local.at[u]) for u in range(n)
    ]
    copies.append(pltpu.make_async_copy(small, region(small_full, place.at, (), 0, small.shape[0]), local.at[n]))
    for copy in copies:
        copy.start()
    parts = []
    for u in range(n):
        rows = units[u] // 2
        base = pl.multiple_of(place.core * rows, rows)
        parts.append(
            [
                Gather(place, own[u].at[pl.ds(base + start, count)], full[u], ORDERS[p], base + start, count, half,
                       send.at[u, p], recv.at[u, p], True)
                for p, (start, count, half) in enumerate(CUTS[rows])
            ]
        )
    rows = small.shape[0]
    parts[0].append(
        Gather(place, small, small_full, ORDERS[0], 0, rows, rows // 2, small_send, small_recv, False)
    )

    def first(u, phase):
        for part in parts[u]:
            part.first(phase)

    def second(u, phase):
        for part in parts[u]:
            part.second(phase)

    def third(u, phase):
        for part in parts[u]:
            part.third(phase)

    def whole(u, phase):
        first(u, phase)
        second(u, phase)
        third(u, phase)

    units_all = range(n)
    for u in units_all:
        first(u, 0)
    for u in units_all:
        second(u, 0)
    for u in units_all:
        third(u, 0)
    for copy in copies:
        copy.wait()
    if plan == "all":
        for phase in (1, 2):
            for u in units_all:
                first(u, phase)
            for u in units_all:
                second(u, phase)
            for u in units_all:
                third(u, phase)
    if plan == "mixed":
        whole(0, 1)
        first(0, 2)
        for u in range(n):
            if u + 1 < n:
                whole(u + 1, 1)
            second(u, 2)
            if u + 1 < n:
                first(u + 1, 2)
            third(u, 2)
    if plan == "mixed2":
        first(0, 1)
        second(0, 1)
        first(1, 1)
        third(0, 1)
        first(0, 2)
        for u in range(n):
            if u + 1 < n:
                second(u + 1, 1)
            if u + 2 < n:
                first(u + 2, 1)
            if u + 1 < n:
                third(u + 1, 1)
            second(u, 2)
            if u + 1 < n:
                first(u + 1, 2)
            third(u, 2)
    if plan == "serial":
        for u in range(n):
            for phase in range(3):
                whole(u, phase)
    elif plan == "early":
        for u in range(n):
            whole(u, 0)
            whole(u, 1)
        first(0, 2)
        for u in range(n):
            second(u, 2)
            if u + 1 < n:
                first(u + 1, 2)
            third(u, 2)
    elif plan == "pipe":
        whole(0, 0)
        whole(0, 1)
        first(0, 2)
        for u in range(n):
            if u + 1 < n:
                whole(u + 1, 0)
                whole(u + 1, 1)
            second(u, 2)
            if u + 1 < n:
                first(u + 1, 2)
            third(u, 2)
    for unit in parts:
        for part in unit:
            part.finish()


def gather_all(own, small, plan, collective_id):
    units = [a.shape[0] for a in own]
    n = len(units)
    any_space = pl.BlockSpec(memory_space=pl.ANY)
    shapes = [jax.ShapeDtypeStruct((RING, RING, RING) + a.shape, a.dtype) for a in (*own, small)]
    return pl.pallas_call(
        functools.partial(gather_kernel, units, plan),
        out_shape=shapes,
        in_specs=[pl.BlockSpec(memory_space=pltpu.VMEM)] * (n + 1),
        out_specs=[any_space] * (n + 1),
        scratch_shapes=[
            pltpu.SemaphoreType.DMA((n, 3, 3, 8)),
            pltpu.SemaphoreType.DMA((n, 3, 3, 8)),
            pltpu.SemaphoreType.DMA((3, 4)),
            pltpu.SemaphoreType.DMA((3, 4)),
            pltpu.SemaphoreType.DMA((n + 1,)),
        ],
        compiler_params=pltpu.CompilerParams(collective_id=collective_id, has_side_effects=True),
        name="gather_weights",
    )(*own, small)


def blockwise(ref_shape, body):
    lead = ref_shape[:-2]
    total = 1
    for size in lead:
        total *= size
    if total == 1:
        body((0,) * len(lead))
        return

    def step(i, _):
        index = (i // lead[1], i % lead[1]) if len(lead) == 2 else (i,)
        body(index)
        return 0

    lax.fori_loop(0, total, step, 0)


def add_into(dst, *others):
    def body(index):
        total = dst[index].astype(jnp.float32)
        for other in others:
            total = total + other[index].astype(jnp.float32)
        dst[index] = total.astype(dst.dtype)

    blockwise(dst.shape, body)


class Scatter:
    def __init__(self, place, order, grads, own, twin, half_in, full_in, out, base, other, start, count, half, sems):
        self.place, self.order = place, order
        self.grads, self.own, self.twin, self.half_in, self.full_in, self.out = grads, own, twin, half_in, full_in, out
        self.base, self.other, self.start, self.count, self.half = base, other, start, count, half
        self.send, self.recv, self.near, self.far_send, self.far_recv, self.out_send, self.out_recv = sems
        self.sent = []
        self.twins = {}

    def piece(self, ref, phase, by, start, count):
        at = self.place.shifted(self.order[2 - phase], by)
        return region(ref, at, self.order[: 2 - phase], start, count)

    def bring(self, k, by):
        src = self.piece(self.grads, 0, by, self.base + self.start, self.count)
        near = pltpu.make_async_copy(src, self.piece(self.own, 0, by, self.start, self.count), self.near.at[k])
        near.start()
        away = self.piece(self.grads, 0, by, self.other + self.start, self.count)
        far = remote(away, self.piece(self.twin, 0, by, self.start, self.count), self.far_send.at[k],
                     self.far_recv.at[k], self.place.sibling())
        far.start()
        self.twins[by] = (near, far)

    def join(self, by):
        near, far = self.twins[by]
        near.wait()
        far.wait()
        add_into(self.piece(self.own, 0, by, self.start, self.count), self.piece(self.twin, 0, by, self.start, self.count))

    def incoming(self, refs, phase, start, count):
        lead = (slice(None),) * (2 - phase)
        return refs[phase].at[lead + (pl.ds(start, count),)]

    def push(self, phase, i, src, dst, by):
        copy = remote(src, dst, self.send.at[phase, i], self.recv.at[phase, i],
                      self.place.neighbour(self.order[2 - phase], by))
        copy.start()
        self.sent.append(copy)
        return copy

    def halves(self):
        return ((self.start, self.half), (self.start + self.half, self.count - self.half))

    def opposite(self, phase):
        if phase == 0:
            self.join(2)
        self.now = [
            self.push(phase, i, self.piece(self.own, phase, 2, start, count),
                      self.incoming(self.half_in, phase, start, count), by)
            for i, (by, (start, count)) in enumerate(zip((1, -1), self.halves()))
        ]
        if phase == 0:
            self.join(1)
            self.join(-1)

    def sides(self, phase):
        later = []
        for i, (by, (start, count)) in enumerate(zip((1, -1), self.halves())):
            self.now[i].wait_recv()
            add_into(self.piece(self.own, phase, by, start, count), self.incoming(self.half_in, phase, start, count))
            lead = (slice(None),) * (2 - phase)
            later.append(
                self.push(phase, 2 + i, self.piece(self.own, phase, by, self.start, self.count),
                          self.full_in[phase].at[(i,) + lead + (pl.ds(self.start, self.count),)], by)
            )
        self.now = later
        if phase == 0:
            self.join(0)

    def centre(self, phase):
        for copy in self.now:
            copy.wait_recv()
        lead = (slice(None),) * (2 - phase)
        rows = (pl.ds(self.start, self.count),)
        mine = self.piece(self.own, phase, 0, self.start, self.count)
        arrived = [self.full_in[phase].at[(i,) + lead + rows] for i in range(2)]
        if phase < 2:
            add_into(mine, *arrived)
            return
        total = mine[...].astype(jnp.float32)
        for ref in arrived:
            total = total + ref[...].astype(jnp.float32)
        rows = pl.ds(self.base + self.start, self.count)
        self.out[rows, :] = total
        self.shown = remote(self.out.at[rows], self.out.at[rows], self.out_send, self.out_recv, self.place.sibling())
        self.shown.start()

    def finish(self):
        for copy in self.sent:
            copy.wait_send()
        self.shown.wait()


def scatter_kernel(units, *refs):
    n = len(units)
    grads, outs = refs[:n], refs[n : 2 * n]
    scratch = refs[2 * n :]
    place = Place()
    place.greet()
    parts = []
    for u in range(n):
        rows = units[u] // 2
        own, twin, h0, h1, h2, f0, f1, f2, send, recv, near, far_send, far_recv, out_send, out_recv = scratch[15 * u : 15 * (u + 1)]
        base = pl.multiple_of(place.core * rows, rows)
        other = pl.multiple_of((1 - place.core) * rows, rows)
        parts.append(
            [
                Scatter(place, ORDERS[p], grads[u], own, twin, (h0, h1, h2), (f0, f1, f2), outs[u], base, other,
                        start, count, half,
                        (send.at[p], recv.at[p], near.at[p], far_send.at[p], far_recv.at[p], out_send.at[p], out_recv.at[p]))
                for p, (start, count, half) in enumerate(CUTS[rows])
            ]
        )
    every = [part for unit in parts for part in unit]
    for k, by in enumerate((2, 1, -1, 0)):
        for part in every:
            part.bring(k, by)
    for phase in range(3):
        for part in every:
            part.opposite(phase)
        for part in every:
            part.sides(phase)
        for part in every:
            part.centre(phase)
    for part in every:
        part.finish()


def scatter_units(grads, collective_id):
    units = [g.shape[3] for g in grads]
    n = len(units)
    scratch = []
    for size in units:
        rows = size // 2
        block = (rows, 256)
        dma = pltpu.SemaphoreType.DMA
        scratch += [pltpu.VMEM((RING,) * 3 + block, jnp.bfloat16)] * 2
        scratch += [pltpu.VMEM((RING,) * (2 - t) + block, jnp.bfloat16) for t in range(3)]
        scratch += [pltpu.VMEM((2,) + (RING,) * (2 - t) + block, jnp.bfloat16) for t in range(3)]
        scratch += [dma((3, 3, 4)), dma((3, 3, 4)), dma((3, 4)), dma((3, 4)), dma((3, 4)), dma((3,)), dma((3,))]
    return pl.pallas_call(
        functools.partial(scatter_kernel, units),
        out_shape=[jax.ShapeDtypeStruct((size, 256), jnp.float32) for size in units],
        in_specs=[pl.BlockSpec(memory_space=pl.ANY)] * n,
        out_specs=[pl.BlockSpec(memory_space=pltpu.VMEM)] * n,
        scratch_shapes=scratch,
        compiler_params=pltpu.CompilerParams(
            collective_id=collective_id, has_side_effects=True, vmem_limit_bytes=58 * 2**20
        ),
        name="scatter_grads",
    )(*grads)


HEAD = 64
SEQ = 197
ROWS = 208
WIDTH = 1024
HEADS = 16
FF_BLOCK = 256
QKV = 192
EPS = 1e-06
VMEM_LIMIT = 48 * 2**20


def wide(block):
    return jnp.concatenate([block[i] for i in range(RING)], axis=1)


def store_blocks(ref, value):
    for i in range(RING):
        ref[0, 0, i] = value[:, i * 256 : (i + 1) * 256].astype(ref.dtype)


def feature_row(small_ref, row):
    return jnp.concatenate([small_ref[0, 0, i, row : row + 1, :] for i in range(RING)], axis=1)


def dot_nt(a, b):
    return lax.dot_general(a, b, (((1,), (1,)), ((), ())), preferred_element_type=jnp.float32)


def dot_nn(a, b):
    return lax.dot_general(a, b, (((1,), (0,)), ((), ())), preferred_element_type=jnp.float32)


def dot_tn(a, b):
    return lax.dot_general(a, b, (((0,), (0,)), ((), ())), preferred_element_type=jnp.float32)


def norm_parts(x):
    average = jnp.mean(x, axis=1, keepdims=True)
    centered = x - average
    inverse = lax.rsqrt(jnp.mean(centered * centered, axis=1, keepdims=True) + EPS)
    return centered * inverse, inverse


def norm_back(incoming, x, gain):
    normed, inverse = norm_parts(x)
    scaled = incoming * gain
    mean = jnp.mean(scaled, axis=1, keepdims=True)
    along = jnp.mean(scaled * normed, axis=1, keepdims=True)
    result = inverse * (scaled - mean - normed * along)
    return result, jnp.sum(incoming * normed, axis=0, keepdims=True), jnp.sum(incoming, axis=0, keepdims=True)


def softmax(queries, keys):
    scores = dot_nt(queries, keys) * HEAD**-0.5
    column = lax.broadcasted_iota(jnp.int32, scores.shape, 1)
    scores = jnp.where(column < SEQ, scores, -1e30)
    highest = jnp.max(scores, axis=1, keepdims=True)
    expon = jnp.exp(scores - highest)
    return expon / jnp.sum(expon, axis=1, keepdims=True)


def attend_forward_kernel(layer, x_ref, small_ref, here_ref, qkv_ref, proj_ref, mid_ref, mixed_ref, att_ref, h_ref):
    step = pl.program_id(0)

    @pl.when(step == 0)
    def _():
        x = x_ref[...].astype(jnp.float32)
        normed, _ = norm_parts(x)
        h_ref[...] = (normed * feature_row(small_ref, 8 * layer) + feature_row(small_ref, 8 * layer + 2)).astype(jnp.bfloat16)
        mid_ref[...] = x + feature_row(small_ref, 8 * layer + 4)

    bias = here_ref[0, 0, 0, 8 * layer + 7 : 8 * layer + 8, :QKV]
    mixed = (dot_nt(h_ref[...], wide(qkv_ref[0, 0])) + bias).astype(jnp.bfloat16)
    mixed_ref[0] = mixed
    probs = softmax(mixed[:, :HEAD], mixed[:, HEAD : 2 * HEAD]).astype(jnp.bfloat16)
    att = dot_nn(probs, mixed[:, 2 * HEAD :]).astype(jnp.bfloat16)
    att_ref[0] = att
    mid_ref[...] += dot_nn(att, wide(proj_ref[0, 0]))


def feed_forward_kernel(layer, mid_ref, small_ref, here_ref, up_ref, down_ref, out_ref, upward_ref, h_ref):
    step = pl.program_id(0)

    @pl.when(step == 0)
    def _():
        mid = mid_ref[...]
        normed, _ = norm_parts(mid)
        h_ref[...] = (normed * feature_row(small_ref, 8 * layer + 1) + feature_row(small_ref, 8 * layer + 3)).astype(jnp.bfloat16)
        out_ref[...] = mid + feature_row(small_ref, 8 * layer + 5)

    upward = dot_nt(h_ref[...], wide(up_ref[0, 0])) + here_ref[0, 0, 0, 8 * layer + 6 : 8 * layer + 7, :]
    upward_ref[0] = upward
    activated = (upward * (0.5 + 0.5 * lax.erf(upward * 2**-0.5))).astype(jnp.bfloat16)
    out_ref[...] += dot_nn(activated, wide(down_ref[0, 0]))


def feed_back_kernel(layer, g_ref, mid_ref, small_ref, upward_ref, up_ref, down_ref, gmid_ref, grad_ref, bias_ref, rows_ref, h_ref, low_ref, acc_ref):
    step = pl.program_id(0)

    @pl.when(step == 0)
    def _():
        normed, _ = norm_parts(mid_ref[...])
        h_ref[...] = (normed * feature_row(small_ref, 8 * layer + 1) + feature_row(small_ref, 8 * layer + 3)).astype(jnp.bfloat16)
        low_ref[...] = g_ref[...].astype(jnp.bfloat16)
        acc_ref[...] = jnp.zeros_like(acc_ref)

    low = low_ref[...]
    upward = upward_ref[0]
    phi_total = 0.5 + 0.5 * lax.erf(upward * 2**-0.5)
    density = jnp.exp(-0.5 * upward * upward) * (2 * jnp.pi) ** -0.5
    activated = (upward * phi_total).astype(jnp.bfloat16)
    g_up = (dot_nt(low, wide(down_ref[0, 0])) * (phi_total + upward * density)).astype(jnp.bfloat16)
    store_blocks(grad_ref.at[:, :, :, FF_BLOCK:], dot_tn(activated, low))
    store_blocks(grad_ref.at[:, :, :, :FF_BLOCK], dot_tn(g_up, h_ref[...]))
    bias_ref[0] = jnp.sum(g_up.astype(jnp.float32), axis=0, keepdims=True)
    acc_ref[...] += dot_nn(g_up, wide(up_ref[0, 0]))

    @pl.when(step == pl.num_programs(0) - 1)
    def _():
        part, gain, shift = norm_back(acc_ref[...], mid_ref[...], feature_row(small_ref, 8 * layer + 1))
        gmid_ref[...] = g_ref[...].astype(jnp.float32) + part
        rows_ref[0:1, :] = jnp.sum(low_ref[...].astype(jnp.float32), axis=0, keepdims=True)
        rows_ref[1:2, :] = gain
        rows_ref[2:3, :] = shift


def attend_back_kernel(layer, g_ref, x_ref, small_ref, mixed_ref, att_ref, qkv_ref, proj_ref, gx_ref, grad_ref, bias_ref, rows_ref, h_ref, low_ref, acc_ref):
    step = pl.program_id(0)

    @pl.when(step == 0)
    def _():
        normed, _ = norm_parts(x_ref[...].astype(jnp.float32))
        h_ref[...] = (normed * feature_row(small_ref, 8 * layer) + feature_row(small_ref, 8 * layer + 2)).astype(jnp.bfloat16)
        low_ref[...] = g_ref[...].astype(jnp.bfloat16)
        acc_ref[...] = jnp.zeros_like(acc_ref)

    low = low_ref[...]
    mixed = mixed_ref[0]
    queries, keys, values = mixed[:, :HEAD], mixed[:, HEAD : 2 * HEAD], mixed[:, 2 * HEAD :]
    store_blocks(grad_ref.at[:, :, :, QKV:], dot_tn(att_ref[0], low))
    g_att = dot_nt(low, wide(proj_ref[0, 0])).astype(jnp.bfloat16)
    probs = softmax(queries, keys)
    g_probs = dot_nt(g_att, values)
    g_values = dot_tn(probs.astype(jnp.bfloat16), g_att)
    centre = jnp.sum(probs * g_probs, axis=1, keepdims=True)
    g_scores = (probs * (g_probs - centre) * HEAD**-0.5).astype(jnp.bfloat16)
    g_mixed = jnp.concatenate([dot_nn(g_scores, keys), dot_tn(g_scores, queries), g_values], axis=1).astype(jnp.bfloat16)
    store_blocks(grad_ref.at[:, :, :, :QKV], dot_tn(g_mixed, h_ref[...]))
    bias_ref[0, :, :QKV] = jnp.sum(g_mixed.astype(jnp.float32), axis=0, keepdims=True)
    acc_ref[...] += dot_nn(g_mixed, wide(qkv_ref[0, 0]))

    @pl.when(step == pl.num_programs(0) - 1)
    def _():
        part, gain, shift = norm_back(acc_ref[...], x_ref[...].astype(jnp.float32), feature_row(small_ref, 8 * layer))
        gx_ref[...] = g_ref[...] + part
        rows_ref[0:1, :] = jnp.sum(low_ref[...].astype(jnp.float32), axis=0, keepdims=True)
        rows_ref[1:2, :] = gain
        rows_ref[2:3, :] = shift


def whole_spec(shape):
    return pl.BlockSpec(shape, lambda i: (0,) * len(shape))


def block_spec(rows, at):
    return pl.BlockSpec((1, 1, RING, rows, 256), lambda i: (i // RING, i % RING, 0, at, 0))


TOKENS_SPEC = whole_spec((ROWS, WIDTH))
SMALL_SPEC = pl.BlockSpec((1, 1, RING, 16, 256), lambda i: (0, 0, 0, 0, 0))
HERE_SPEC = pl.BlockSpec((1, 1, 1, 16, 256), lambda i: (i // RING, i % RING, 0, 0, 0))


def saved_spec(width):
    return pl.BlockSpec((1, ROWS, width), lambda i: (i, 0, 0))


def saved(width, dtype):
    return jax.ShapeDtypeStruct((HEADS, ROWS, width), dtype)


def compute(kernel, out_shape, in_specs, out_specs, scratch, name):
    return pl.pallas_call(
        kernel,
        grid=(HEADS,),
        out_shape=out_shape,
        in_specs=in_specs,
        out_specs=out_specs,
        scratch_shapes=scratch,
        compiler_params=pltpu.CompilerParams(vmem_limit_bytes=VMEM_LIMIT),
        name=name,
    )


TOKENS_F32 = jax.ShapeDtypeStruct((ROWS, WIDTH), jnp.float32)
LOW = pltpu.VMEM((ROWS, WIDTH), jnp.bfloat16)
FULL = pltpu.VMEM((ROWS, WIDTH), jnp.float32)


def attend_forward(layer, x, small, weights):
    return compute(
        functools.partial(attend_forward_kernel, layer),
        [TOKENS_F32, saved(QKV, jnp.bfloat16), saved(HEAD, jnp.bfloat16)],
        [TOKENS_SPEC, SMALL_SPEC, HERE_SPEC, block_spec(QKV, 0), block_spec(HEAD, 3)],
        [TOKENS_SPEC, saved_spec(QKV), saved_spec(HEAD)],
        [LOW],
        "attend_forward",
    )(x, small, small, weights, weights)


def feed_forward(layer, mid, small, weights):
    return compute(
        functools.partial(feed_forward_kernel, layer),
        [TOKENS_F32, saved(FF_BLOCK, jnp.float32)],
        [TOKENS_SPEC, SMALL_SPEC, HERE_SPEC, block_spec(FF_BLOCK, 0), block_spec(FF_BLOCK, 1)],
        [TOKENS_SPEC, saved_spec(FF_BLOCK)],
        [LOW],
        "feed_forward",
    )(mid, small, small, weights, weights)


def grads_shape(rows):
    return jax.ShapeDtypeStruct((RING, RING, RING, rows, 256), jnp.bfloat16)


BIAS_SHAPE = jax.ShapeDtypeStruct((HEADS, 1, 256), jnp.float32)
BIAS_SPEC = pl.BlockSpec((1, 1, 256), lambda i: (i, 0, 0))
SUMS_SHAPE = jax.ShapeDtypeStruct((8, WIDTH), jnp.float32)
SUMS_SPEC = whole_spec((8, WIDTH))


def feed_back(layer, g, mid, small, upward, weights):
    return compute(
        functools.partial(feed_back_kernel, layer),
        [TOKENS_F32, grads_shape(2 * FF_BLOCK), BIAS_SHAPE, SUMS_SHAPE],
        [TOKENS_SPEC, TOKENS_SPEC, SMALL_SPEC, saved_spec(FF_BLOCK), block_spec(FF_BLOCK, 0), block_spec(FF_BLOCK, 1)],
        [TOKENS_SPEC, block_spec(2 * FF_BLOCK, 0), BIAS_SPEC, SUMS_SPEC],
        [LOW, LOW, FULL],
        "feed_back",
    )(g, mid, small, upward, weights, weights)


def attend_back(layer, g, x, small, mixed, att, weights):
    return compute(
        functools.partial(attend_back_kernel, layer),
        [TOKENS_F32, grads_shape(QKV + HEAD), BIAS_SHAPE, SUMS_SHAPE],
        [TOKENS_SPEC, TOKENS_SPEC, SMALL_SPEC, saved_spec(QKV), saved_spec(HEAD), block_spec(QKV, 0), block_spec(HEAD, 3)],
        [TOKENS_SPEC, block_spec(QKV + HEAD, 0), BIAS_SPEC, SUMS_SPEC],
        [LOW, LOW, FULL],
        "attend_back",
    )(g, x, small, mixed, att, weights, weights)


def to_images(rows):
    padded = jnp.pad(rows.reshape(3, SEQ, 256), ((0, 1), (0, ROWS - SEQ), (0, 0)))
    return lax.all_to_all(padded, "row", 0, 0)


def from_images(image):
    parts = image.astype(jnp.bfloat16).reshape(ROWS, RING, 256).transpose(1, 0, 2)
    back = lax.all_to_all(parts, "row", 0, 0)
    return back[:3, :SEQ].reshape(3 * SEQ, 256).astype(jnp.float32)


def as_tokens(blocks):
    return blocks.transpose(1, 0, 2).reshape(ROWS, WIDTH)


def shards(tokens, norm_gain, norm_shift, qkv_weight, qv_bias, proj_weight, proj_bias, up_weight, up_bias, down_weight, down_bias, cotangent):
    layers = qkv_weight.shape[0]
    own, small = [], []
    for layer in range(layers):
        own.append(jnp.concatenate([qkv_weight[layer].T, proj_weight[layer]], axis=0))
        own.append(jnp.concatenate([up_weight[layer].T, down_weight[layer]], axis=0))
        qv = qv_bias[layer]
        zeros = jnp.zeros((HEAD,), jnp.float32)
        qkv_row = jnp.concatenate([qv[:HEAD], zeros, qv[HEAD:], zeros])
        small.append(
            jnp.stack([norm_gain[layer, 0], norm_gain[layer, 1], norm_shift[layer, 0], norm_shift[layer, 1],
                       proj_bias[layer], down_bias[layer], up_bias[layer], qkv_row])
        )
    *full, small = gather_all(own, jnp.concatenate(small), "mixed2", 0)
    x = as_tokens(to_images(tokens)).astype(jnp.float32)
    g = as_tokens(to_images(cotangent.astype(jnp.bfloat16))).astype(jnp.float32)
    kept = []
    for layer in range(layers):
        mid, mixed, att = attend_forward(layer, x, small, full[2 * layer])
        out, upward = feed_forward(layer, mid, small, full[2 * layer + 1])
        kept.append((x, mid, mixed, att, upward))
        x = out
    encoded = from_images(x)
    weight_grads, sums = [None] * layers, [None] * layers
    for layer in reversed(range(layers)):
        x, mid, mixed, att, upward = kept[layer]
        g_mid, feed_grad, up_sums, feed_rows = feed_back(layer, g, mid, small, upward, full[2 * layer + 1])
        g, attend_grad, qkv_sums, attend_rows = attend_back(layer, g_mid, x, small, mixed, att, full[2 * layer])
        weight_grads[layer] = scatter_units((feed_grad, attend_grad), 1)
        sums[layer] = jnp.concatenate(
            [up_sums.reshape(-1), qkv_sums.reshape(-1), feed_rows[:3].reshape(-1), attend_rows[:3].reshape(-1)]
        )
    grad_tokens = from_images(g)
    sums = lax.psum(jnp.stack(sums), ("dp", "row", "col"))
    row, col = lax.axis_index("row"), lax.axis_index("col")
    up_sums = lax.dynamic_slice_in_dim(sums[:, : 16 * 256].reshape(layers, 16, 256), col, 1, 1)[:, 0]
    qkv_sums = lax.dynamic_slice_in_dim(sums[:, 16 * 256 : 32 * 256].reshape(layers, 16, 256), col, 1, 1)[:, 0]
    features = lax.dynamic_slice_in_dim(sums[:, 32 * 256 :].reshape(layers, 6, RING, 256), row, 1, 2)[:, :, 0]
    feed = [weight_grads[layer][0] for layer in range(layers)]
    attend = [weight_grads[layer][1] for layer in range(layers)]
    return (
        encoded,
        grad_tokens,
        jnp.stack([features[:, 4], features[:, 1]], axis=1),
        jnp.stack([features[:, 5], features[:, 2]], axis=1),
        jnp.stack([a[:QKV].T for a in attend]),
        jnp.concatenate([qkv_sums[:, :HEAD], qkv_sums[:, 2 * HEAD : QKV]], axis=1),
        jnp.stack([a[QKV:] for a in attend]),
        features[:, 3],
        jnp.stack([f[:FF_BLOCK].T for f in feed]),
        up_sums,
        jnp.stack([f[FF_BLOCK:] for f in feed]),
        features[:, 0],
    )


def solution(mesh):
    in_specs = (
        P(("dp", "col"), "row"),
        P(None, None, "row"),
        P(None, None, "row"),
        P(None, "row", "col"),
        P(None, "col"),
        P(None, "col", "row"),
        P(None, "row"),
        P(None, "row", "col"),
        P(None, "col"),
        P(None, "col", "row"),
        P(None, "row"),
        P(("dp", "col"), "row"),
    )
    out_specs = (
        P(("dp", "col"), "row"),
        P(("dp", "col"), "row"),
        P(None, None, "row"),
        P(None, None, "row"),
        P(None, "row", "col"),
        P(None, "col"),
        P(None, "col", "row"),
        P(None, "row"),
        P(None, "row", "col"),
        P(None, "col"),
        P(None, "col", "row"),
        P(None, "row"),
    )
    return jax.shard_map(shards, mesh=mesh, in_specs=in_specs, out_specs=out_specs, check_vma=False)
```

time: 2360 us -> 679 us (0.29)
  blocking collectives: 905 us -> 0 us
  waiting for transfers between devices: 950 us -> 145 us
  Pallas kernels: 0 us -> 461 us
  matrix products: 162 us -> 0 us
  local copies, waits for them, and re-layouts: 188 us -> 32.1 us
  other arithmetic: 100 us -> 6.76 us
    unnamed x10 -> x0, blocking collectives: 746 us -> none
    all_gather x16 -> x0, waiting for transfers between devices: 695 us -> none  [the longest x8 411 us: col_then_row(): gathered = lax.all_gather(local, 'col', axis=0, tiled=True)]
    pallas_call x0 -> x11, Pallas kernels: none -> 461 us  [the longest x2 154 us: scatter_units(): pl.pallas_call(functools.partial(scatter_kernel, units), out_shape=[jax.S...]
    unnamed x38 -> x1, waiting for transfers between devices: 255 us -> 0.02 us
    dot_general x36 -> x0, matrix products: 162 us -> none  [the longest x16 91.5 us: contract(): lax.dot_general(left_rows, matrix, (((1,), (inner,)), ((), ())), preferre...]
    psum x13 -> x0, blocking collectives: 159 us -> none  [the longest x1 67.2 us: shards(): lax.psum((jnp.stack([gain_in, gain_mid]), jnp.stack([shift_in, shift_mid]...]
    psum x2 -> x1, waiting for transfers between devices: 0.01 us -> 138 us  [shards(): sums = lax.psum(jnp.stack(sums), ('dp', 'row', 'col'))]
    unnamed x158 -> x33, local copies, waits for them, and re-layouts: 140 us -> 8.02 us
  transfers between devices with their start and end apart: 34 -> 5, of which waited for: 25 -> 2; matrix products, arithmetic and copies ran while one was open for 10% -> 4% of each run, Pallas kernels for 0% -> 19%
where the time goes in v1:
time: 679 us; the launch traced here: 676 us
  Pallas kernels  461 us (68%)
  waiting for transfers between devices  145 us (21%)
  local copies, waits for them, and re-layouts  32.1 us (5%)
  starting transfers between devices  16.4 us (2%)
  between operations  14.4 us (2%)
    pallas_call x2, Pallas kernels, scatter_units(): pl.pallas_call(functools.partial(scatter_kernel, units), out_shape=[jax.S...  154 us
    psum x1, waiting for transfers between devices, shards(): sums = lax.psum(jnp.stack(sums), ('dp', 'row', 'col'))  138 us
    pallas_call x1, Pallas kernels, gather_all(): pl.pallas_call(functools.partial(gather_kernel, units, plan), out_shape=s...  132 us
    pallas_call x2, Pallas kernels, attend_back(): compute(functools.partial(attend_back_kernel, layer), [TOKENS_F32, grads_...  51 us
    pallas_call x2, Pallas kernels, feed_back(): compute(functools.partial(feed_back_kernel, layer), [TOKENS_F32, grads_sh...  48 us
    pallas_call x2, Pallas kernels, attend_forward(): compute(functools.partial(attend_forward_kernel, layer), [TOKENS_F32, sav...  42.3 us
    pallas_call x2, Pallas kernels, feed_forward(): compute(functools.partial(feed_forward_kernel, layer), [TOKENS_F32, saved...  34.6 us
  transfers between devices with their start and end apart: 5, of which 2 were waited for; matrix products, arithmetic and copies ran while one was open for 4% of the time, Pallas kernels for 19%

profile of v1, /device:TPU:1, one launch (start us, length us, event | category | flops | bytes accessed | tf_op | source)
XLA Modules:
  0.0 675.7 jit_solution(2277020376335036164)
XLA Ops:
  9.0 4.8 all-to-all-start
  18.5 1.1 convert_element_type.44
  22.1 1.2 concatenate.36.refs_4_
  25.1 4.2 all-to-all-start.2
  30.1 131.5 %gather_weights.1 = (bf16[4,4,4,256,256]{4,3,2,1,0:T(8,128)(2,1)}, bf16[4,4,4,512,256]{4,3,2,1,0:T(8,128)(2,1)}, bf16[4,4,4,256,256]{4,3,2,1,0:T(8,128)(2,1)}, b...) custom-call(bf16[256,256]{1,0:T(8,128)(2,1)} %get-tuple-element.172.refs_0_, ...), custom_call_target="tpu_custom_call" | custom-call | tf_op jit(solution)/shard_map/gather_weights/pallas_call | solution.py:241
  162.0 1.2 copy-done
  163.2 21.1 %attend_forward.2 = (f32[208,1024]{1,0:T(8,128)S(1)}, bf16[16,208,192]{2,1,0:T(8,128)(2,1)S(1)}, bf16[16,208,64]{2,1,0:T(8,128)(2,1)S(1)}) custom-call(f32[208,1024]{1,0:T(8,128)S(1)} %bitcast.113, f32[4,4,4,16,256]{4,3,2,1,0:T(8,128)S(1)} %copy-done, f32[4,4,4,16,256]{4,3,2,1,0:T(8,128)S(1)} %copy-done, ...), custom_call_target="tpu_custom_call" | custom-call | tf_op jit(solution)/shard_map/attend_forward/pallas_call | solution.py:638
  185.3 17.3 %feed_forward.2 = (f32[208,1024]{1,0:T(8,128)S(1)}, f32[16,208,256]{2,1,0:T(8,128)S(1)}) custom-call(f32[208,1024]{1,0:T(8,128)S(1)} %get-tuple-element.49.mid_ref, f32[4,4,4,16,256]{4,3,2,1,0:T(8,128)S(1)} %copy-done, f32[4,4,4,16,256]{4,3,2,1,0:T(8,128)S(1)} %copy-done, bf16[4,4,4,512,256]{4,3,2,1,0:T(8,128)(2,1)} %get-tuple-element.50.up_ref.down_ref, ...), custom_call_target="tpu_custom_call" | custom-call | tf_op jit(solution)/shard_map/feed_forward/pallas_call | solution.py:649
  202.6 1.7 copy-done.2
  204.3 21.1 %attend_forward.3 = (f32[208,1024]{1,0:T(8,128)S(1)}, bf16[16,208,192]{2,1,0:T(8,128)(2,1)S(1)}, bf16[16,208,64]{2,1,0:T(8,128)(2,1)S(1)}) custom-call(f32[208,1024]{1,0:T(8,128)S(1)} %get-tuple-element.51.x_ref, f32[4,4,4,16,256]{4,3,2,1,0:T(8,128)S(1)} %copy-done, f32[4,4,4,16,256]{4,3,2,1,0:T(8,128)S(1)} %copy-done, ...), custom_call_target="tpu_custom_call" | custom-call | tf_op jit(solution)/shard_map/attend_forward/pallas_call | solution.py:638
  225.5 17.3 %feed_forward.3 = (f32[208,1024]{1,0:T(8,128)S(1)}, f32[16,208,256]{2,1,0:T(8,128)S(1)}) custom-call(f32[208,1024]{1,0:T(8,128)S(1)} %get-tuple-element.53.mid_ref, f32[4,4,4,16,256]{4,3,2,1,0:T(8,128)S(1)} %copy-done, f32[4,4,4,16,256]{4,3,2,1,0:T(8,128)S(1)} %copy-done, bf16[4,4,4,512,256]{4,3,2,1,0:T(8,128)(2,1)} %get-tuple-element.54.up_ref.down_ref, ...), custom_call_target="tpu_custom_call" | custom-call | tf_op jit(solution)/shard_map/feed_forward/pallas_call | solution.py:649
  242.8 1.7 copy-done.3
  244.5 24.1 %feed_back.2 = (f32[208,1024]{1,0:T(8,128)S(1)}, bf16[4,4,4,512,256]{4,3,2,1,0:T(8,128)(2,1)}, f32[16,1,256]{2,1,0:T(1,128)S(1)}, f32[8,1024]{1,0:T(8,128)S(1)}) custom-call(f32[208,1024]{1,0:T(8,128)S(1)} %bitcast.115, f32[208,1024]{1,0:T(8,128)S(1)} %get-tuple-element.53.mid_ref, f32[4,4,4,16,256]{4,3,2,1,0:T(8,128)S(1)} %copy-done, ...), custom_call_target="tpu_custom_call" | custom-call | tf_op jit(solution)/shard_map/feed_back/pallas_call | solution.py:670
  268.6 25.6 %attend_back.2 = (f32[208,1024]{1,0:T(8,128)S(1)}, bf16[4,4,4,256,256]{4,3,2,1,0:T(8,128)(2,1)}, f32[16,1,256]{2,1,0:T(1,128)S(1)}, f32[8,1024]{1,0:T(8,128)S(1)}) custom-call(f32[208,1024]{1,0:T(8,128)S(1)} %get-tuple-element.57.g_ref, f32[208,1024]{1,0:T(8,128)S(1)} %get-tuple-element.51.x_ref, f32[4,4,4,16,256]{4,3,2,1,0:T(8,128)S(1)} %copy-done, ...), custom_call_target="tpu_custom_call" | custom-call | tf_op jit(solution)/shard_map/attend_back/pallas_call | solution.py:681
  294.2 77.2 %scatter_grads.3 = (f32[512,256]{1,0:T(8,128)}, f32[256,256]{1,0:T(8,128)}) custom-call(bf16[4,4,4,512,256]{4,3,2,1,0:T(8,128)(2,1)} %get-tuple-element.77.refs_0_, bf16[4,4,4,256,256]{4,3,2,1,0:T(8,128)(2,1)} %get-tuple-element.78.refs_1_), custom_call_target="tpu_custom_call" | custom-call | tf_op jit(solution)/shard_map/scatter_grads/pallas_call | solution.py:425
  371.5 1.6 slice_bitcast_fusion.4
  373.1 1.5 slice_bitcast_fusion.10
  374.6 23.9 %feed_back.3 = (f32[208,1024]{1,0:T(8,128)S(1)}, bf16[4,4,4,512,256]{4,3,2,1,0:T(8,128)(2,1)}, f32[16,1,256]{2,1,0:T(1,128)S(1)}, f32[8,1024]{1,0:T(8,128)S(1)}) custom-call(f32[208,1024]{1,0:T(8,128)S(1)} %get-tuple-element.60.g_ref, f32[208,1024]{1,0:T(8,128)S(1)} %get-tuple-element.49.mid_ref, f32[4,4,4,16,256]{4,3,2,1,0:T(8,128)S(1)} %copy-done.1, ...), custom_call_target="tpu_custom_call" | custom-call | tf_op jit(solution)/shard_map/feed_back/pallas_call | solution.py:670
  398.5 25.4 %attend_back.3 = (f32[208,1024]{1,0:T(8,128)S(1)}, bf16[4,4,4,256,256]{4,3,2,1,0:T(8,128)(2,1)}, f32[16,1,256]{2,1,0:T(1,128)S(1)}, f32[8,1024]{1,0:T(8,128)S(1)}) custom-call(f32[208,1024]{1,0:T(8,128)S(1)} %get-tuple-element.62.g_ref, f32[208,1024]{1,0:T(8,128)S(1)} %bitcast.114, f32[4,4,4,16,256]{4,3,2,1,0:T(8,128)S(1)} %copy-done.1, ...), custom_call_target="tpu_custom_call" | custom-call | tf_op jit(solution)/shard_map/attend_back/pallas_call | solution.py:681
  423.9 76.6 %scatter_grads.2 = (f32[512,256]{1,0:T(8,128)}, f32[256,256]{1,0:T(8,128)}) custom-call(bf16[4,4,4,512,256]{4,3,2,1,0:T(8,128)(2,1)} %get-tuple-element.74.refs_0_, bf16[4,4,4,256,256]{4,3,2,1,0:T(8,128)(2,1)} %get-tuple-element.75.refs_1_), custom_call_target="tpu_custom_call" | custom-call | tf_op jit(solution)/shard_map/scatter_grads/pallas_call | solution.py:425
  503.2 3.5 all-to-all-start.1
  513.7 137.7 %all-reduce.4.cloned.1.call-done = f32[2,14336]{1,0:T(2,128)} async-done(((f32[2,14336]{1,0:T(2,128)}), f32[2,14336]{1,0:T(2,128)}) %all-reduce.4.cloned.1.call-update) | async-done | bytes 114704 | tf_op jit(solution)/shard_map/psum | solution.py:739
  655.5 3.8 all-to-all-start.3
  660.8 7.1 %all-to-all-done.3 = bf16[4,208,256]{2,1,0:T(8,128)(2,1)S(1)} async-done(((bf16[4,208,256]{2,1,0:T(8,128)(2,1)}), bf16[4,208,256]{2,1,0:T(8,128)(2,1)S(1)}, u32[]{:S(2)}, u32[]{:S(2)}) %all-to-all-start.3) | async-done | bytes 426016 | tf_op jit(solution)/shard_map/all_to_all | solution.py:698
  (94 shorter events, 28.8 us)
Async XLA Ops:
  9.0 16.1 %all-to-all-start = ((bf16[4,208,256]{2,1,0:T(8,128)(2,1)}), bf16[4,208,256]{2,1,0:T(8,128)(2,1)S(1)}, u32[]{:S(2)}, u32[]{:S(2)}) async-start(bf16[4,208,256]{2,1,0:T(8,128)(2,1)} %pad.7), calls=%async_computation | async-start | bytes 851968 | tf_op jit(solution)/shard_map/all_to_all | solution.py:693
  25.1 136.7 %all-to-all-start.2 = ((bf16[4,208,256]{2,1,0:T(8,128)(2,1)}), bf16[4,208,256]{2,1,0:T(8,128)(2,1)S(1)}, u32[]{:S(2)}, u32[]{:S(2)}) async-start(bf16[4,208,256]{2,1,0:T(8,128)(2,1)} %pad.8), calls=%async_computation.2 | async-start | bytes 851968 | tf_op jit(solution)/shard_map/all_to_all | solution.py:693
  162.0 1.2 copy-start
  184.4 0.9 copy-start.6
  202.6 1.7 copy-start.2
  242.8 1.7 copy-start.3
  244.5 24.1 %copy-start.4 = (f32[208,1024]{1,0:T(8,128)}, f32[208,1024]{1,0:T(8,128)S(1)}, u32[]{:S(2)}) copy-start(f32[208,1024]{1,0:T(8,128)S(1)} %get-tuple-element.55) | copy-start | bytes 2555908
  294.2 80.3 %copy-start.1 = (f32[4,4,4,16,256]{4,3,2,1,0:T(8,128)S(1)}, f32[4,4,4,16,256]{4,3,2,1,0:T(8,128)}, u32[]{:S(2)}) copy-start(f32[4,4,4,16,256]{4,3,2,1,0:T(8,128)} %get-tuple-element.47.small_ref.here_ref) | copy-start | bytes 3145732
  374.6 23.9 %copy-start.7 = (bf16[16,208,64]{2,1,0:T(8,128)(2,1)S(1)}, bf16[16,208,64]{2,1,0:T(8,128)(2,1)}, u32[]{:S(2)}) copy-start(bf16[16,208,64]{2,1,0:T(8,128)(2,1)} %copy-done.6) | copy-start | bytes 1277956
  398.5 25.4 %copy-start.8 = (f32[8,1024]{1,0:T(8,128)}, f32[8,1024]{1,0:T(8,128)S(1)}, u32[]{:S(2)}) copy-start(f32[8,1024]{1,0:T(8,128)S(1)} %get-tuple-element.68) | copy-start | bytes 98308
  423.9 76.6 %copy-start.10 = (f32[8,1024]{1,0:T(8,128)}, f32[8,1024]{1,0:T(8,128)S(1)}, u32[]{:S(2)}) copy-start(f32[8,1024]{1,0:T(8,128)S(1)} %get-tuple-element.69) | copy-start | bytes 98308
  423.9 78.5 %copy-start.5 = (f32[208,1024]{1,0:T(8,128)S(1)}, f32[208,1024]{1,0:T(8,128)}, u32[]{:S(2)}) copy-start(f32[208,1024]{1,0:T(8,128)} %copy-done.4) | copy-start | bytes 2555908
  423.9 83.7 %copy-start.9 = (f32[8,1024]{1,0:T(8,128)S(1)}, f32[8,1024]{1,0:T(8,128)}, u32[]{:S(2)}) copy-start(f32[8,1024]{1,0:T(8,128)} %copy-done.8) | copy-start | bytes 98308
  423.9 84.5 %copy-start.12 = (f32[512,256]{1,0:T(8,128)S(1)}, f32[512,256]{1,0:T(8,128)}, u32[]{:S(2)}) copy-start(f32[512,256]{1,0:T(8,128)} %get-tuple-element.81) | copy-start | bytes 1572868
  423.9 85.6 %copy-start.11 = (f32[1,256,192]{1,2,0:T(8,128)S(1)}, f32[1,256,192]{1,2,0:T(8,128)}, u32[]{:S(2)}) copy-start(f32[1,256,192]{1,2,0:T(8,128)} %slice_bitcast_fusion.4) | copy-start | bytes 589828
  500.5 10.7 %copy-start.13 = (f32[1,64,256]{2,1,0:T(8,128)S(1)}, f32[1,64,256]{2,1,0:T(8,128)}, u32[]{:S(2)}) copy-start(f32[1,64,256]{2,1,0:T(8,128)} %slice_bitcast_fusion.10) | copy-start | bytes 196612
  503.2 152.3 %all-to-all-start.1 = ((bf16[4,208,256]{2,1,0:T(8,128)(2,1)}), bf16[4,208,256]{2,1,0:T(8,128)(2,1)S(1)}, u32[]{:S(2)}, u32[]{:S(2)}) async-start(bf16[4,208,256]{2,1,0:T(8,128)(2,1)} %bitcast.111), calls=%async_computation.1 | async-start | bytes 851968 | tf_op jit(solution)/shard_map/all_to_all | solution.py:698
  506.7 144.7 %all-reduce.4.cloned.1.call-start = ((), (), s32[]{:S(2)}) async-start(), calls=%async_computation.4 | async-start | bytes 229376 | tf_op jit(solution)/shard_map/psum | solution.py:739
  655.5 12.4 %all-to-all-start.3 = ((bf16[4,208,256]{2,1,0:T(8,128)(2,1)}), bf16[4,208,256]{2,1,0:T(8,128)(2,1)S(1)}, u32[]{:S(2)}, u32[]{:S(2)}) async-start(bf16[4,208,256]{2,1,0:T(8,128)(2,1)} %bitcast.109), calls=%async_computation.3 | async-start | bytes 851968 | tf_op jit(solution)/shard_map/all_to_all | solution.py:698
Sparse Core Ops, SparseCore 0:
  512.8 138.5 all-reduce.3

commit v2 on v0

v2 whole, which is shorter than its diff:
```python
import functools

import jax
import jax.numpy as jnp
from jax import lax
from jax.experimental import pallas as pl
from jax.experimental.pallas import tpu as pltpu
from jax.sharding import PartitionSpec as P

MESH = pl.DeviceIdType.MESH
RING = 4
STEPS = 4
AXES = "yzx"
ORDERS = (("x", "y", "z"), ("y", "z", "x"), ("z", "x", "y"))
KINDS = 3
UNIT = 256
CORE = 128
CUTS = (((0, 48), (48, 48), (96, 32)), ((0, 48), (48, 32), (80, 48)), ((0, 32), (32, 48), (80, 48)))
NEAR = tuple((axis, by) for axis in "xyz" for by in (1, -1)) + (("core", 1),)
ROW_PEERS = (("x", 1), ("x", 2), ("x", -1))
VMEM_LIMIT = 60 * 2**20
DMA = pltpu.SemaphoreType.DMA
ANY = pl.BlockSpec(memory_space=pl.ANY)
VMEM = pl.BlockSpec(memory_space=pltpu.VMEM)
BF16 = jnp.bfloat16
F32 = jnp.float32


def number(kind, layer):
    return 2 * kind + layer


class Place:
    def __init__(self):
        self.core = lax.axis_index("dp")
        block = lax.axis_index("col")
        self.at = {"x": lax.axis_index("row"), "y": block // RING, "z": block % RING}
        self.mine = pl.ds(pl.multiple_of(self.core * CORE, CORE), CORE)
        self.other = pl.ds(pl.multiple_of((1 - self.core) * CORE, CORE), CORE)

    def shifted(self, axis, by):
        moved = dict(self.at)
        moved[axis] = (self.at[axis] + by + RING) % RING
        return moved

    def neighbour(self, axis, by):
        if axis == "core":
            return (1 - self.core, self.at["x"], self.at["y"] * RING + self.at["z"])
        at = self.shifted(axis, by)
        return (self.core, at["x"], at["y"] * RING + at["z"])

    def sibling(self):
        return self.neighbour("core", 1)

    def tell(self, semaphore, peers):
        for axis, by in peers:
            pl.semaphore_signal(semaphore, inc=1, device_id=self.neighbour(axis, by), device_id_type=MESH)

    def greet(self, peers):
        barrier = pltpu.get_barrier_semaphore()
        self.tell(barrier, peers)
        pl.semaphore_wait(barrier, len(peers))


def region(ref, axes, at, whole, start, count):
    index = tuple(pl.ds(0, RING) if a in whole else at[a] for a in axes)
    return ref.at[index + (pl.ds(start, count),)]


def remote(src, dst, send, recv, device):
    return pltpu.make_async_remote_copy(
        src_ref=src, dst_ref=dst, send_sem=send, recv_sem=recv, device_id=device, device_id_type=MESH
    )


class Ring:
    def __init__(self, place, full, units, order, phase, start, count, half, send, recv, own=None):
        self.place, self.full, self.units, self.own = place, full, units, own
        self.axis, self.whole = order[phase], order[:phase]
        self.start, self.count = start, count
        self.halves = ((start, half), (start + half, count - half))
        self.send, self.recv = send, recv

    def piece(self, by, start, count):
        at = self.place.shifted(self.axis, by)
        index = tuple(pl.ds(0, RING) if a in self.whole else at[a] for a in AXES)
        return self.full.at[(self.units,) + index + (pl.ds(start, count),)]

    def to(self, i):
        return self.place.neighbour(self.axis, (1, -1)[i])

    def whole_copy(self, i):
        here = self.piece(0, self.start, self.count)
        return remote(here if self.own is None else self.own, here, self.send.at[i], self.recv.at[i], self.to(i))

    def half_copy(self, i):
        ref = self.piece((-1, 1)[i], *self.halves[i])
        return remote(ref, ref, self.send.at[2 + i], self.recv.at[2 + i], self.to(i))

    def share(self, k):
        ref = self.piece((-1, 1)[k], self.start, self.count) if k < 2 else self.piece(2, *self.halves[k - 2])
        return remote(ref, ref, self.send.at[4 + k], self.recv.at[4 + k], self.place.sibling())

    def share_all(self):
        index = tuple(pl.ds(0, RING) if a in self.whole + (self.axis,) else self.place.at[a] for a in AXES)
        ref = self.full.at[(self.units,) + index + (pl.ds(self.start, self.count),)]
        return remote(ref, ref, self.send.at[4], self.recv.at[4], self.place.sibling())

    def first(self):
        for i in range(2):
            self.whole_copy(i).start()

    def second(self):
        for i in range(2):
            self.whole_copy(i).wait_recv()
            self.half_copy(i).start()

    def third(self):
        for i in range(2):
            self.half_copy(i).wait_recv()

    def finish(self):
        for i in range(2):
            self.whole_copy(i).wait_send()
            self.half_copy(i).wait_send()


class Gather:
    def __init__(self, place, own, full, small_own, small_full, sems):
        one_send, one_recv, two_send, two_recv, three_send, three_recv, small_send, small_recv = sems
        self.one, self.two, self.three = [], {}, {}
        base = pl.multiple_of(place.core * CORE, CORE)
        for kind in range(KINDS):
            for p, (start, count) in enumerate(CUTS[kind]):
                rows = base + start
                self.one.append(
                    Ring(place, full, pl.ds(2 * kind, 2), ORDERS[p], 0, rows, count, 16, one_send.at[kind, p],
                         one_recv.at[kind, p], own.at[pl.ds(2 * kind, 2), pl.ds(rows, count)])
                )
            for layer in range(2):
                u = number(kind, layer)
                for phase, into, send, recv in ((1, self.two, two_send, two_recv), (2, self.three, three_send, three_recv)):
                    into[u] = [
                        Ring(place, full, u, ORDERS[p], phase, base + start, count,
                             count // 2 if count == 32 else (16, 32)[(p + layer) % 2], send.at[u, p], recv.at[u, p])
                        for p, (start, count) in enumerate(CUTS[kind])
                    ]
        rows = small_own.shape[1]
        self.small = [
            Ring(place, small_full, pl.ds(0, 1), ORDERS[0], phase, 0, rows, rows // 2, small_send.at[phase],
                 small_recv.at[phase], small_own if phase == 0 else None)
            for phase in range(3)
        ]

    def begin(self):
        rings = self.one + [self.small[0]]
        for name in ("first", "second", "third"):
            for ring in rings:
                getattr(ring, name)()

    def small_phase(self, phase, name):
        getattr(self.small[phase], name)()

    def first_two(self, u):
        for ring in self.two[u]:
            ring.first()

    def second_two(self, u):
        for ring in self.two[u]:
            ring.second()

    def third_two(self, u):
        for ring in self.two[u]:
            ring.third()

    def first_three(self, u):
        for ring in self.three[u]:
            ring.first()
        for ring in self.two[u]:
            ring.share_all().start()

    def second_three(self, u):
        for ring in self.three[u]:
            ring.second()
        for ring in self.three[u]:
            for k in range(2):
                ring.share(k).start()

    def third_three(self, u):
        for ring in self.three[u]:
            ring.third()
            for k in range(2, 4):
                ring.share(k).start()

    def ready(self, u):
        for ring in self.two[u]:
            ring.share_all().wait()
            ring.finish()
        for ring in self.three[u]:
            for k in range(4):
                ring.share(k).wait()
            ring.finish()

    def finish(self):
        for ring in self.one + self.small:
            ring.finish()


def gather_semaphores():
    return [DMA((KINDS, 3, 4)), DMA((KINDS, 3, 4)), DMA((6, 3, 5)), DMA((6, 3, 5)), DMA((6, 3, 8)), DMA((6, 3, 8)),
            DMA((3, 4)), DMA((3, 4))]


def blockwise(shape, body):
    lead = shape[:-2]
    if not lead:
        body(())
        return

    def step(i, _):
        body((i // lead[1], i % lead[1]) if len(lead) == 2 else (i,))
        return 0

    total = 1
    for size in lead:
        total *= size
    lax.fori_loop(0, total, step, 0)


def add_to(dst, first, *others):
    def body(index):
        if len(others) == 1 and dst.dtype == BF16:
            dst[index] = first[index] + others[0][index]
            return
        total = first[index].astype(F32)
        for other in others:
            total = total + other[index].astype(F32)
        dst[index] = total.astype(dst.dtype)

    blockwise(dst.shape, body)


class Fold:
    def __init__(self, place, order, phase, work, half_in, full_in, dst, start, count, half, send, recv):
        self.place, self.work, self.half_in, self.full_in, self.dst = place, work, half_in, full_in, dst
        self.axis, self.whole = order[2 - phase], order[: 2 - phase]
        self.axes = tuple(a for a in AXES if a not in order[3 - phase :])
        self.start, self.count = start, count
        self.halves = ((start, half), (start + half, count - half))
        self.send, self.recv = send, recv
        self.lead = (slice(None),) * (2 - phase)

    def piece(self, by, start, count, ref=None):
        ref = self.work if ref is None else ref
        return region(ref, self.axes, self.place.shifted(self.axis, by), self.whole, start, count)

    def half_copy(self, i):
        src = self.piece(2, *self.halves[i])
        dst = self.half_in.at[self.lead + (pl.ds(*self.halves[i]),)]
        return remote(src, dst, self.send.at[i], self.recv.at[i], self.place.neighbour(self.axis, (1, -1)[i]))

    def arrived(self, i):
        return self.full_in.at[(i,) + self.lead + (pl.ds(self.start, self.count),)]

    def whole_copy(self, i):
        by = (1, -1)[i]
        src = self.piece(by, self.start, self.count)
        return remote(src, self.arrived(i), self.send.at[2 + i], self.recv.at[2 + i], self.place.neighbour(self.axis, by))

    def opposite(self):
        for i in range(2):
            self.half_copy(i).start()

    def sides(self):
        for i in range(2):
            self.half_copy(i).wait_recv()
            ref = self.piece((1, -1)[i], *self.halves[i])
            add_to(ref, ref, self.half_in.at[self.lead + (pl.ds(*self.halves[i]),)])
            self.whole_copy(i).start()

    def centre(self):
        for i in range(2):
            self.whole_copy(i).wait_recv()
        add_to(self.dst, self.piece(0, self.start, self.count), self.arrived(0), self.arrived(1))

    def finish(self):
        for i in range(2):
            self.half_copy(i).wait_send()
            self.whole_copy(i).wait_send()


class Scatter:
    def __init__(self, place, kind, layer, stage, first, second, third, out, result, sems):
        self.place, self.stage = place, stage
        self.work, self.twin, reduced, inner = first[0], first[1], second[0], third[0]
        self.out, self.result = out, result
        (self.near, self.far_send, self.far_recv, send, recv, self.show_send, self.show_recv, self.local) = sems
        base = pl.multiple_of(place.core * CORE, CORE)

        def parts(phase, work, half_in, full_in, dst_of):
            return [
                Fold(place, ORDERS[p], phase, work, half_in, full_in, dst_of(start, count), start, count,
                     count // 2 if count == 32 else (16, 32)[(p + layer) % 2], send.at[phase, p], recv.at[phase, p])
                for p, (start, count) in enumerate(CUTS[kind])
            ]

        self.one = parts(0, self.work, first[2], first[3], lambda start, count: reduced.at[:, :, pl.ds(start, count)])
        self.two = parts(1, reduced, second[1], second[2], lambda start, count: inner.at[:, pl.ds(start, count)])
        self.three = parts(2, inner, third[1], third[2], lambda start, count: out.at[pl.ds(base + start, count)])

    def stay(self, step):
        slot = step % 2
        return pltpu.make_async_copy(self.stage.at[slot, :, :, self.place.mine], self.work.at[step], self.near.at[slot])

    def go(self, step):
        slot = step % 2
        return remote(self.stage.at[slot, :, :, self.place.other], self.twin.at[step], self.far_send.at[slot],
                      self.far_recv.at[step], self.place.sibling())

    def free(self, step):
        self.stay(step).wait()
        self.go(step).wait_send()

    def hand_over(self, step):
        self.stay(step).start()
        self.go(step).start()

    def handed(self):
        for step in (STEPS - 2, STEPS - 1):
            self.free(step)
        for step in range(STEPS):
            self.go(step).wait_recv()

    def join(self, *which):
        for by in which:
            for part in self.one:
                ref = part.piece(by, part.start, part.count)
                add_to(ref, ref, part.piece(by, part.start, part.count, self.twin))

    def each(self, name, parts):
        for part in parts:
            getattr(part, name)()

    def show(self):
        ref = self.out.at[self.place.mine]
        return remote(ref, ref, self.show_send, self.show_recv, self.place.sibling())

    def keep(self):
        return pltpu.make_async_copy(self.out, self.result, self.local)

    def open(self):
        self.handed()
        self.join(2)
        self.each("opposite", self.one)
        self.join(1, -1)

    def sides_one(self):
        self.each("sides", self.one)
        self.join(0)

    def centre_one(self):
        self.each("centre", self.one)
        self.each("finish", self.one)

    def start_two(self):
        self.each("opposite", self.two)

    def sides_two(self):
        self.each("sides", self.two)

    def centre_two(self):
        self.each("centre", self.two)
        self.each("opposite", self.three)

    def sides_three(self):
        self.each("sides", self.three)

    def centre_three(self):
        self.each("centre", self.three)
        self.show().start()
        self.each("finish", self.two)
        self.each("finish", self.three)

    def finish(self):
        self.show().wait()
        self.keep().start()
        self.keep().wait()


def first_buffers():
    blocks = (RING,) * 3 + (CORE, 256)
    return [pltpu.VMEM(blocks, BF16), pltpu.VMEM(blocks, BF16), pltpu.VMEM(blocks[1:], BF16), pltpu.VMEM((2,) + blocks[1:], BF16)]


def later_buffers():
    def some(*lead):
        return pltpu.VMEM(lead + (CORE, 256), BF16)

    return [some(RING, RING), some(RING), some(2, RING), some(RING), some(), some(2)]


def scatter_semaphores():
    return [DMA((2,)), DMA((2,)), DMA((STEPS,)), DMA((3, 3, 4)), DMA((3, 3, 4)), DMA, DMA, DMA]


class Turn:
    def __init__(self, place, src, dst, send, recv, local):
        self.place, self.src, self.dst, self.send, self.recv, self.local = place, src, dst, send, recv, local

    def copies(self):
        row = self.place.at["x"]
        return [
            remote(self.src.at[self.place.shifted("x", by)["x"]], self.dst.at[row], self.send.at[k], self.recv.at[k],
                   self.place.neighbour("x", by))
            for k, (_, by) in enumerate(ROW_PEERS)
        ]

    def own(self):
        row = self.place.at["x"]
        return pltpu.make_async_copy(self.src.at[row], self.dst.at[row], self.local)

    def start(self):
        self.own().start()
        for copy in self.copies():
            copy.start()

    def end(self):
        self.own().wait()
        for copy in self.copies():
            copy.wait()


TURN_SEMAPHORES = [DMA((3,)), DMA((3,)), DMA]


class Total:
    def __init__(self, place, mine, out, result, slots, core_in, send, recv, core_sems):
        self.place, self.mine, self.out, self.result, self.slots = place, mine, out, result, slots
        self.send, self.recv, self.core_in, self.core_sems = send, recv, core_in, core_sems
        rows = mine.shape[0] // 2
        self.half = pl.ds(pl.multiple_of(place.core * rows, rows), rows)
        self.away = pl.ds(pl.multiple_of((1 - place.core) * rows, rows), rows)

    def core_copy(self):
        return remote(self.mine.at[self.away], self.core_in, self.core_sems.at[0], self.core_sems.at[1], self.place.sibling())

    def copies(self, k):
        axis = "xyz"[k]
        slot = self.slots.at[k, self.place.at[axis]]
        return [
            remote(slot, slot, self.send.at[k, j], self.recv.at[k, j], self.place.neighbour(axis, by))
            for j, by in enumerate((1, 2, -1))
        ]

    def start(self):
        self.core_copy().start()

    def core_sum(self):
        self.core_copy().wait_recv()
        self.put(0, self.mine[self.half] + self.core_in[...])

    def put(self, k, value):
        self.slots[k, self.place.at["xyz"[k]]] = value
        for copy in self.copies(k):
            copy.start()

    def take(self, k):
        for copy in self.copies(k):
            copy.wait_recv()
        return (self.slots[k, 0] + self.slots[k, 1]) + (self.slots[k, 2] + self.slots[k, 3])

    def out_copy(self):
        ref = self.out.at[self.half]
        return remote(ref, ref, self.core_sems.at[2], self.core_sems.at[3], self.place.sibling())

    def last(self):
        self.out[self.half] = self.take(2)
        self.out_copy().start()

    def finish(self):
        self.core_copy().wait_send()
        for k in range(3):
            for copy in self.copies(k):
                copy.wait_send()
        self.out_copy().wait()
        copy = pltpu.make_async_copy(self.out, self.result, self.core_sems.at[4])
        copy.start()
        copy.wait()


def total_buffers(rows):
    return [pltpu.VMEM((rows, 1024), F32), pltpu.VMEM((3, RING, rows // 2, 1024), F32), pltpu.VMEM((rows // 2, 1024), F32),
            DMA((3, 3)), DMA((3, 3)), DMA((5,))]


TOTAL_PEERS = NEAR + tuple((axis, 2) for axis in "xyz")


HEAD = 64
SEQ = 197
ROWS = 208
WIDTH = 1024
BLOCKS = RING
FF_HALF = 128
QKV = 192
EPS = 1e-06
SMALL = 16
SUM_ROWS = 32
LAYER_SUMS = 14


def wide(block):
    return jnp.concatenate([block[i] for i in range(RING)], axis=1)


def tall(ref, start, rows):
    return jnp.concatenate([wide(ref[j, :, start : start + rows, :]) for j in range(BLOCKS)], axis=0)


def as_rows(ref):
    return wide(ref[...]).astype(F32)


def put_rows(ref, value):
    for i in range(RING):
        ref[i] = value[:, i * 256 : (i + 1) * 256].astype(ref.dtype)


def store_blocks(stage, slot, start, value):
    rows = value.shape[0] // BLOCKS
    for j in range(BLOCKS):
        for i in range(RING):
            block = value[j * rows : (j + 1) * rows, i * 256 : (i + 1) * 256]
            stage[slot, j, i, start : start + rows, :] = block.astype(stage.dtype)


def feature_row(small, layer, row):
    return jnp.concatenate([small[0, 0, 0, i, 8 * layer + row : 8 * layer + row + 1, :] for i in range(RING)], axis=1)


def here_row(small, step, layer, row, start, width):
    at = 8 * layer + row
    return jnp.concatenate([small[0, step, j, 0, at : at + 1, start : start + width] for j in range(BLOCKS)], axis=1)


def dot_nt(a, b):
    return lax.dot_general(a, b, (((1,), (1,)), ((), ())), preferred_element_type=F32)


def dot_nn(a, b):
    return lax.dot_general(a, b, (((1,), (0,)), ((), ())), preferred_element_type=F32)


def dot_tn(a, b):
    return lax.dot_general(a, b, (((0,), (0,)), ((), ())), preferred_element_type=F32)


def norm_parts(x):
    average = jnp.mean(x, axis=1, keepdims=True)
    centered = x - average
    inverse = lax.rsqrt(jnp.mean(centered * centered, axis=1, keepdims=True) + EPS)
    return centered * inverse, inverse


def norm_low(x, small, layer, j):
    normed, _ = norm_parts(x)
    return (normed * feature_row(small, layer, j) + feature_row(small, layer, 2 + j)).astype(BF16)


def norm_back(incoming, x, gain):
    normed, inverse = norm_parts(x)
    scaled = incoming * gain
    mean = jnp.mean(scaled, axis=1, keepdims=True)
    along = jnp.mean(scaled * normed, axis=1, keepdims=True)
    result = inverse * (scaled - mean - normed * along)
    return result, jnp.sum(incoming * normed, axis=0, keepdims=True), jnp.sum(incoming, axis=0, keepdims=True)


def softmax(queries, keys):
    scores = dot_nt(queries, keys) * HEAD**-0.5
    column = lax.broadcasted_iota(jnp.int32, scores.shape, 1)
    scores = jnp.where(column < SEQ, scores, -1e30)
    highest = jnp.max(scores, axis=1, keepdims=True)
    expon = jnp.exp(scores - highest)
    return expon * (1.0 / jnp.sum(expon, axis=1, keepdims=True))


def head_parts(mixed, j):
    at = j * QKV
    return mixed[:, at : at + HEAD], mixed[:, at + HEAD : at + 2 * HEAD], mixed[:, at + 2 * HEAD : at + QKV]


class Stream:
    def __init__(self, pairs, sems):
        self.pairs, self.sems = pairs, sems

    def copies(self, step):
        slot = step % 2
        return [
            pltpu.make_async_copy(source(step), slots.at[slot], self.sems.at[slot, k])
            for k, (source, slots) in enumerate(self.pairs)
        ]

    def start(self, step):
        for copy in self.copies(step):
            copy.start()

    def run(self, body, hooks):
        def one(step, _):
            for copy in self.copies(step):
                copy.wait()

            @pl.when(step + 1 < STEPS)
            def _():
                self.start(step + 1)

            body(step, step % 2)
            for at in sorted(hooks):
                @pl.when(step == at)
                def _(at=at):
                    for act in hooks[at]:
                        act()
            return 0

        self.start(0)
        lax.fori_loop(0, STEPS, one, 0)


ORDER = [(0, 0), (1, 0), (2, 0), (0, 1), (1, 1), (2, 1)]
SAVED = [
    jax.ShapeDtypeStruct((2, STEPS, ROWS, BLOCKS * QKV), BF16),
    jax.ShapeDtypeStruct((2, STEPS, ROWS, BLOCKS * HEAD), BF16),
    jax.ShapeDtypeStruct((2, STEPS, BLOCKS, ROWS, ROWS), BF16),
    jax.ShapeDtypeStruct((2, 2, STEPS, ROWS, BLOCKS * FF_HALF), BF16),
    jax.ShapeDtypeStruct((2, 2, STEPS, ROWS, BLOCKS * FF_HALF), BF16),
]
TOKENS = jax.ShapeDtypeStruct((ROWS, WIDTH), F32)
TURNED = jax.ShapeDtypeStruct((RING, ROWS, 256), BF16)
WEIGHTS = jax.ShapeDtypeStruct((6, RING, RING, RING, UNIT, 256), BF16)
SMALLS = jax.ShapeDtypeStruct((1, RING, RING, RING, SMALL, 256), F32)


def scratch_like(shape):
    return pltpu.VMEM(shape.shape, shape.dtype)


def forward_kernel(own_ref, small_ref, tokens_ref, cotangent_ref, full, small_out, x0_out, g_out, mid_out, x1_out, end_out,
                   mixed_out, att_out, probs_out, act_out, slope_out,
                   small, x0, resid, low, acc, mids, ends, slots, mixed_all, att_all, probs_all, act_all, slope_all, *sems):
    place = Place()
    turn_x, turn_g = Turn(place, tokens_ref, x0, *sems[0:3]), Turn(place, cotangent_ref, g_out, *sems[3:6])
    load, saves, misc = sems[6:9]
    gather = Gather(place, own_ref, full, small_ref, small, sems[9:])
    units = [number(*pair) for pair in ORDER]

    own_copies = [
        pltpu.make_async_copy(own_ref.at[:, place.mine],
                              full.at[:, place.at["y"], place.at["z"], place.at["x"], place.mine], misc.at[0]),
        pltpu.make_async_copy(small_ref, small.at[:, place.at["y"], place.at["z"], place.at["x"]], misc.at[1]),
    ]
    for copy in own_copies:
        copy.start()
    place.greet(NEAR + (("x", 2),))
    gather.begin()
    turn_x.start()
    for copy in own_copies:
        copy.wait()
    gather.small_phase(1, "first")
    gather.first_two(units[0])
    gather.second_two(units[0])
    gather.small_phase(1, "second")
    gather.first_two(units[1])
    gather.third_two(units[0])
    gather.first_three(units[0])
    gather.small_phase(1, "third")
    gather.small_phase(2, "first")
    gather.second_two(units[1])
    gather.first_two(units[2])
    gather.third_two(units[1])
    gather.small_phase(2, "second")
    gather.second_three(units[0])
    gather.first_three(units[1])
    gather.small_phase(2, "third")
    turn_x.end()
    resid[...] = as_rows(x0)
    gather.third_three(units[0])
    gather.ready(units[0])
    kept = []

    def keep(src, dst, k):
        copy = pltpu.make_async_copy(src, dst, misc.at[k])
        copy.start()
        kept.append((src, dst, k))

    keep(x0, x0_out, 2)
    keep(small, small_out, 3)
    turn_g.start()

    for k, (kind, layer) in enumerate(ORDER):
        unit = units[k]
        hooks = {0: [], 1: [], 3: []}
        if k + 2 < 6:
            hooks[0] += [functools.partial(gather.second_two, units[k + 2])]
            if k + 3 < 6:
                hooks[0] += [functools.partial(gather.first_two, units[k + 3])]
            hooks[0] += [functools.partial(gather.third_two, units[k + 2])]
        if k + 1 < 6:
            hooks[1] += [functools.partial(gather.second_three, units[k + 1])]
            if k + 2 < 6:
                hooks[1] += [functools.partial(gather.first_three, units[k + 2])]
            hooks[3] += [functools.partial(gather.third_three, units[k + 1]), functools.partial(gather.ready, units[k + 1])]

        def save(which, src, dst, step):
            return pltpu.make_async_copy(src, dst, saves.at[which, k, step])

        if kind == 0:
            low[...] = norm_low(resid[...], small, layer, 0)
            acc[...] = resid[...] + feature_row(small, layer, 4)

            def body(step, slot):
                weights = slots.at[slot]
                mixed = dot_nt(low[...], tall(weights, 0, QKV)) + here_row(small, step, layer, 7, 0, QKV)
                mixed = mixed.astype(BF16)
                mixed_all[layer, step] = mixed
                attended = []
                for j in range(BLOCKS):
                    queries, keys, values = head_parts(mixed, j)
                    probs = softmax(queries, keys).astype(BF16)
                    probs_all[layer, step, j] = probs
                    attended.append(dot_nn(probs, values).astype(BF16))
                attended = jnp.concatenate(attended, axis=1)
                att_all[layer, step] = attended
                acc[...] += dot_nn(attended, tall(weights, QKV, HEAD))
                for copy in copies(step):
                    copy.start()

            def copies(step):
                pairs = ((mixed_all, mixed_out), (att_all, att_out), (probs_all, probs_out))
                return [save(i, src.at[layer, step], dst.at[layer, step], step) for i, (src, dst) in enumerate(pairs)]
        else:
            half = kind - 1
            if half == 0:
                mids[layer] = acc[...]
                resid[...] = acc[...]
                low[...] = norm_low(resid[...], small, layer, 1)
                acc[...] = resid[...] + feature_row(small, layer, 5)
                keep(mids.at[layer], mid_out.at[layer], 4 + layer)

            def body(step, slot):
                weights = slots.at[slot]
                upward = dot_nt(low[...], tall(weights, 0, FF_HALF)) + here_row(small, step, layer, 6, half * FF_HALF, FF_HALF)
                below = 0.5 + 0.5 * lax.erf(upward * 2**-0.5)
                activated = (upward * below).astype(BF16)
                act_all[layer, half, step] = activated
                slope = below + upward * (jnp.exp(-0.5 * upward * upward) * (2 * jnp.pi) ** -0.5)
                slope_all[layer, half, step] = slope.astype(BF16)
                acc[...] += dot_nn(activated, tall(weights, FF_HALF, FF_HALF))
                for copy in copies(step):
                    copy.start()

            def copies(step):
                pairs = ((act_all, act_out), (slope_all, slope_out))
                return [save(i, src.at[layer, half, step], dst.at[layer, half, step], step) for i, (src, dst) in enumerate(pairs)]

        Stream([(lambda step: full.at[unit, step], slots)], load.at[k]).run(body, hooks)
        for step in range(STEPS):
            for copy in copies(step):
                copy.wait()
        if kind == 2 and layer == 0:
            resid[...] = acc[...]
            keep(resid, x1_out, 6)
            pltpu.make_async_copy(resid, x1_out, misc.at[6]).wait()
            kept.pop()
    put_rows(ends, acc[...])
    keep(ends, end_out, 7)
    turn_g.end()
    gather.finish()
    for src, dst, k in kept:
        pltpu.make_async_copy(src, dst, misc.at[k]).wait()


def forward(own, small, tokens, cotangent):
    both = jax.ShapeDtypeStruct((2, ROWS, WIDTH), F32)
    return pl.pallas_call(
        forward_kernel,
        out_shape=[WEIGHTS, SMALLS, TURNED, TURNED, both, TOKENS, TURNED, *SAVED],
        in_specs=[VMEM] * 4,
        out_specs=[ANY] * 12,
        scratch_shapes=[
            scratch_like(SMALLS), scratch_like(TURNED), scratch_like(TOKENS), pltpu.VMEM((ROWS, WIDTH), BF16),
            scratch_like(TOKENS), scratch_like(both), scratch_like(TURNED), pltpu.VMEM((2, RING, RING, UNIT, 256), BF16),
            *[scratch_like(s) for s in SAVED],
            *TURN_SEMAPHORES, *TURN_SEMAPHORES, DMA((6, 2, 1)), DMA((3, 6, STEPS)), DMA((8,)),
            *gather_semaphores(),
        ],
        compiler_params=pltpu.CompilerParams(vmem_limit_bytes=VMEM_LIMIT, collective_id=0, has_side_effects=True),
        name="forward",
    )(own, small, tokens, cotangent)


BACK = [(2, 1), (1, 1), (0, 1), (2, 0), (1, 0), (0, 0)]


def backward_kernel(full, small, x0_ref, g_ref, mid_ref, x1_ref, end_ref, mixed_in, att_in, probs_in, act_in, slope_in,
                    encoded_out, tokens_out, grads_out, sums_out,
                    grad, low, here, acc, turned, sums, columns_all, slots, mixed_two, att_two, probs_two, act_two, slope_two, stage, outs,
                    *rest):
    first = [rest[0:4], rest[4:8]]
    later = [rest[8:14], rest[14:20]]
    total_scratch, sems = rest[20:26], rest[26:]
    place = Place()
    turn_out, turn_g = Turn(place, end_ref, encoded_out, *sems[0:3]), Turn(place, turned, tokens_out, *sems[3:6])
    load, free = sems[6:8]
    unit_sems = [[group.at[k] for group in sems[8:]] for k in range(6)]
    scatters = []
    for k, (kind, layer) in enumerate(BACK):
        scatters.append(
            Scatter(place, kind, layer, stage, first[k % 2], later[k % 2][0:3], later[k % 2][3:6], outs.at[k],
                    grads_out.at[number(kind, layer)], unit_sems[k])
        )
    total = Total(place, sums, total_scratch[0], sums_out, *total_scratch[1:])
    place.greet(TOTAL_PEERS)
    turn_out.start()
    grad[...] = as_rows(g_ref)
    sums[...] = jnp.zeros_like(sums)
    columns_all[...] = jnp.zeros_like(columns_all)

    def leave(k):
        place.tell(free.at[k], NEAR)

    def may(k):
        pl.semaphore_wait(free.at[k], len(NEAR))

    for k, (kind, layer) in enumerate(BACK):
        it = scatters[k]
        hooks = {0: [], 1: [], 2: [], 3: []}
        if k >= 2:
            hooks[0] += [scatters[k - 2].sides_two]
        if k >= 1:
            hooks[1] += [scatters[k - 1].sides_one]
        if k >= 2:
            hooks[1] += [scatters[k - 2].centre_two]
            hooks[2] += [scatters[k - 2].sides_three]
        base = LAYER_SUMS * layer

        def begin(step):
            @pl.when(step >= 2)
            def _():
                it.free(step - 2)

            if k >= 2:
                @pl.when(step == 0)
                def _():
                    may(k)

        if kind == 0:
            x = as_rows(x0_ref) if layer == 0 else x1_ref[...]
            here[...] = norm_low(x, small, layer, 0)
            low[...] = grad[...].astype(BF16)
            acc[...] = jnp.zeros_like(acc)

            def body(step, slot):
                weights = slots.at[slot]
                begin(step)
                g = low[...]
                mixed = mixed_two[slot]
                store_blocks(stage, slot, QKV, dot_tn(att_two[slot], g))
                g_all = dot_nt(g, tall(weights, QKV, HEAD)).astype(BF16)
                g_mixed = []
                for j in range(BLOCKS):
                    queries, keys, values = head_parts(mixed, j)
                    g_att = g_all[:, j * HEAD : (j + 1) * HEAD]
                    probs_low = probs_two[slot, j]
                    probs = probs_low.astype(F32)
                    g_probs = dot_nt(g_att, values)
                    g_values = dot_tn(probs_low, g_att)
                    centre = jnp.sum(probs * g_probs, axis=1, keepdims=True)
                    g_scores = (probs * (g_probs - centre) * HEAD**-0.5).astype(BF16)
                    g_mixed += [dot_nn(g_scores, keys), dot_tn(g_scores, queries), g_values]
                g_mixed = jnp.concatenate([part.astype(BF16) for part in g_mixed], axis=1)
                store_blocks(stage, slot, 0, dot_tn(g_mixed, here[...]))
                it.hand_over(step)
                columns_all[layer, 1, step, :, : BLOCKS * QKV] = jnp.sum(g_mixed.astype(F32), axis=0, keepdims=True)
                acc[...] += dot_nn(g_mixed, tall(weights, 0, QKV))

            pairs = [
                (lambda step: full.at[number(kind, layer), step], slots),
                (lambda step: mixed_in.at[layer, step], mixed_two),
                (lambda step: att_in.at[layer, step], att_two),
                (lambda step: probs_in.at[layer, step], probs_two),
            ]
        else:
            half = kind - 1
            if half == 1:
                here[...] = norm_low(mid_ref[layer], small, layer, 1)
                low[...] = grad[...].astype(BF16)
                acc[...] = jnp.zeros_like(acc)

            def body(step, slot):
                weights = slots.at[slot]
                begin(step)
                g = low[...]
                store_blocks(stage, slot, FF_HALF, dot_tn(act_two[slot], g))
                g_up = (dot_nt(g, tall(weights, FF_HALF, FF_HALF)) * slope_two[slot].astype(F32)).astype(BF16)
                store_blocks(stage, slot, 0, dot_tn(g_up, here[...]))
                it.hand_over(step)
                columns = jnp.sum(g_up.astype(F32), axis=0, keepdims=True)
                for j in range(BLOCKS):
                    at = j * 2 * FF_HALF + half * FF_HALF
                    columns_all[layer, 0, step, :, at : at + FF_HALF] = columns[:, j * FF_HALF : (j + 1) * FF_HALF]
                acc[...] += dot_nn(g_up, tall(weights, 0, FF_HALF))

            pairs = [
                (lambda step: full.at[number(kind, layer), step], slots),
                (lambda step: act_in.at[layer, half, step], act_two),
                (lambda step: slope_in.at[layer, half, step], slope_two),
            ]
        Stream(pairs, load.at[k]).run(body, hooks)
        if kind < 2:
            j = kind
            x = mid_ref[layer] if kind == 1 else (as_rows(x0_ref) if layer == 0 else x1_ref[...])
            part, gain, shift = norm_back(acc[...], x, feature_row(small, layer, j))
            at = base + (8 if kind == 1 else 11)
            sums[at : at + 1, :] = jnp.sum(low[...].astype(F32), axis=0, keepdims=True)
            sums[at + 1 : at + 2, :] = gain
            sums[at + 2 : at + 3, :] = shift
            grad[...] = grad[...] + part
        if k == 5:
            put_rows(turned, grad[...])
            turn_g.start()
            for i in range(2):
                for which in range(2):
                    for step in range(STEPS):
                        at = LAYER_SUMS * i + STEPS * which + step
                        sums[at : at + 1, :] = columns_all[i, which, step]
            total.start()
        it.open()
        if k >= 1:
            scatters[k - 1].centre_one()
        if k >= 2:
            scatters[k - 2].centre_three()
        if 1 <= k <= 5:
            leave(k + 1)
        if k >= 1:
            scatters[k - 1].start_two()
    early, late = scatters[4], scatters[5]
    total.core_sum()
    early.sides_two()
    late.sides_one()
    early.centre_two()
    total.put(1, total.take(0))
    late.centre_one()
    may(6)
    late.start_two()
    early.sides_three()
    total.put(2, total.take(1))
    late.sides_two()
    early.centre_three()
    total.last()
    late.centre_two()
    late.sides_three()
    for it in scatters[:4]:
        it.finish()
    late.centre_three()
    turn_out.end()
    turn_g.end()
    total.finish()
    early.finish()
    late.finish()


def backward(full, small, x0, g, mids, x1, ends, saved):
    saved_two = [pltpu.VMEM((2,) + s.shape[-3 if len(s.shape) == 5 and s.shape[1] == STEPS else -2 :], s.dtype) for s in SAVED]
    semaphores = [pltpu.SemaphoreType.DMA((6,) + (s.shape if hasattr(s, "shape") else ())) for s in scatter_semaphores()]
    return pl.pallas_call(
        backward_kernel,
        out_shape=[TURNED, TURNED, jax.ShapeDtypeStruct((6, UNIT, 256), F32), jax.ShapeDtypeStruct((SUM_ROWS, WIDTH), F32)],
        in_specs=[ANY] + [VMEM] * 6 + [ANY] * 5,
        out_specs=[ANY] * 4,
        scratch_shapes=[
            scratch_like(TOKENS), pltpu.VMEM((ROWS, WIDTH), BF16), pltpu.VMEM((ROWS, WIDTH), BF16), scratch_like(TOKENS),
            scratch_like(TURNED), pltpu.VMEM((SUM_ROWS, WIDTH), F32), pltpu.VMEM((2, 2, STEPS, 1, WIDTH), F32),
            pltpu.VMEM((2, RING, RING, UNIT, 256), BF16),
            *saved_two,
            pltpu.VMEM((2, RING, RING, UNIT, 256), BF16), pltpu.VMEM((6, UNIT, 256), F32),
            *first_buffers(), *first_buffers(), *later_buffers(), *later_buffers(),
            *total_buffers(SUM_ROWS),
            *TURN_SEMAPHORES, *TURN_SEMAPHORES, DMA((6, 2, 4)), pltpu.SemaphoreType.REGULAR((7,)),
            *semaphores,
        ],
        compiler_params=pltpu.CompilerParams(vmem_limit_bytes=VMEM_LIMIT, collective_id=1, has_side_effects=True),
        name="backward",
    )(full, small, x0, g, mids, x1, ends, *saved)


def to_images(rows):
    return jnp.pad(rows.reshape(3, SEQ, 256), ((0, 1), (0, ROWS - SEQ), (0, 0)))


def from_images(turned):
    return turned[:3, :SEQ].reshape(3 * SEQ, 256).astype(F32)


def shards(tokens, norm_gain, norm_shift, qkv_weight, qv_bias, proj_weight, proj_bias, up_weight, up_bias, down_weight, down_bias, cotangent):
    layers = qkv_weight.shape[0]
    attention = jnp.concatenate([qkv_weight.transpose(0, 2, 1), proj_weight], axis=1)
    up = up_weight.transpose(0, 2, 1)
    halves = [jnp.concatenate([part[:, at : at + FF_HALF] for part in (up, down_weight)], axis=1) for at in (0, FF_HALF)]
    own = jnp.concatenate([attention, *halves], axis=0)
    zeros = jnp.zeros((layers, HEAD), F32)
    qkv_row = jnp.concatenate([qv_bias[:, :HEAD], zeros, qv_bias[:, HEAD:], zeros], axis=1)
    small = jnp.stack([norm_gain[:, 0], norm_gain[:, 1], norm_shift[:, 0], norm_shift[:, 1], proj_bias, down_bias, up_bias, qkv_row], axis=1)
    full, small, x0, g, mids, x1, ends, *saved = forward(
        own, small.reshape(1, SMALL, 256), to_images(tokens), to_images(cotangent.astype(BF16))
    )
    encoded, grad_tokens, grads, sums = backward(full, small, x0, g, mids, x1, ends, saved)
    row, col = lax.axis_index("row"), lax.axis_index("col")
    sums = sums[: layers * LAYER_SUMS].reshape(layers, LAYER_SUMS, WIDTH)
    up_sums = lax.dynamic_slice_in_dim(sums[:, 0:4].reshape(layers, 16, 256), col, 1, 1)[:, 0]
    qkv_sums = sums[:, 4:8, : BLOCKS * QKV].reshape(layers, 16, QKV)
    qkv_sums = lax.dynamic_slice_in_dim(qkv_sums, col, 1, 1)[:, 0]
    features = lax.dynamic_slice_in_dim(sums[:, 8:].reshape(layers, 6, RING, 256), row, 1, 2)[:, :, 0]
    attention, first, second = grads[0:2], grads[2:4], grads[4:6]
    return (
        from_images(encoded),
        from_images(grad_tokens),
        jnp.stack([features[:, 4], features[:, 1]], axis=1),
        jnp.stack([features[:, 5], features[:, 2]], axis=1),
        attention[:, :QKV].transpose(0, 2, 1),
        jnp.concatenate([qkv_sums[:, :HEAD], qkv_sums[:, 2 * HEAD : QKV]], axis=1),
        attention[:, QKV:],
        features[:, 3],
        jnp.concatenate([first[:, :FF_HALF], second[:, :FF_HALF]], axis=1).transpose(0, 2, 1),
        up_sums,
        jnp.concatenate([first[:, FF_HALF:], second[:, FF_HALF:]], axis=1),
        features[:, 0],
    )


def solution(mesh):
    in_specs = (
        P(("dp", "col"), "row"),
        P(None, None, "row"),
        P(None, None, "row"),
        P(None, "row", "col"),
        P(None, "col"),
        P(None, "col", "row"),
        P(None, "row"),
        P(None, "row", "col"),
        P(None, "col"),
        P(None, "col", "row"),
        P(None, "row"),
        P(("dp", "col"), "row"),
    )
    out_specs = (
        P(("dp", "col"), "row"),
        P(("dp", "col"), "row"),
        P(None, None, "row"),
        P(None, None, "row"),
        P(None, "row", "col"),
        P(None, "col"),
        P(None, "col", "row"),
        P(None, "row"),
        P(None, "row", "col"),
        P(None, "col"),
        P(None, "col", "row"),
        P(None, "row"),
    )
    return jax.shard_map(shards, mesh=mesh, in_specs=in_specs, out_specs=out_specs, check_vma=False)
```

time: 2360 us -> 389 us (0.16)
  waiting for transfers between devices: 950 us -> 0 us
  blocking collectives: 905 us -> 0 us
  Pallas kernels: 0 us -> 370 us
  local copies, waits for them, and re-layouts: 188 us -> 14.7 us
  matrix products: 162 us -> 0 us
  other arithmetic: 100 us -> 2.65 us
  starting transfers between devices: 25.8 us -> 0 us
    unnamed x10 -> x0, blocking collectives: 746 us -> none
    all_gather x16 -> x0, waiting for transfers between devices: 695 us -> none  [the longest x8 411 us: col_then_row(): gathered = lax.all_gather(local, 'col', axis=0, tiled=True)]
    pallas_call x0 -> x2, Pallas kernels: none -> 370 us  [the longest x1 194 us: backward(): pl.pallas_call(backward_kernel, out_shape=[TURNED, TURNED, jax.ShapeDtype...]
    unnamed x38 -> x0, waiting for transfers between devices: 255 us -> none
    dot_general x36 -> x0, matrix products: 162 us -> none  [the longest x16 91.5 us: contract(): lax.dot_general(left_rows, matrix, (((1,), (inner,)), ((), ())), preferre...]
    psum x13 -> x0, blocking collectives: 159 us -> none  [the longest x1 67.2 us: shards(): lax.psum((jnp.stack([gain_in, gain_mid]), jnp.stack([shift_in, shift_mid]...]
    unnamed x158 -> x33, local copies, waits for them, and re-layouts: 140 us -> 4.06 us
    reduce_sum x22 -> x0, other arithmetic: 39.6 us -> none  [the longest x2 7.76 us: shards(): grad_proj_bias = jnp.sum(att_gathered, axis=0, dtype=jnp.float32)]
  transfers between devices with their start and end apart: 34 -> 0, of which waited for: 25 -> 0; matrix products, arithmetic and copies ran while one was open for 10% -> 0% of each run, Pallas kernels for 0% -> 0%
where the time goes in v2:
time: 389 us; the launch traced here: 388 us
  Pallas kernels  370 us (95%)
  local copies, waits for them, and re-layouts  14.7 us (4%)
    pallas_call x1, Pallas kernels, backward(): pl.pallas_call(backward_kernel, out_shape=[TURNED, TURNED, jax.ShapeDtype...  194 us
    pallas_call x1, Pallas kernels, forward(): pl.pallas_call(forward_kernel, out_shape=[WEIGHTS, SMALLS, TURNED, TURNED...  176 us

profile of v2, /device:TPU:1, one launch (start us, length us, event | category | flops | bytes accessed | tf_op | source)
XLA Modules:
  0.0 388.2 jit_solution(17800034417847819318)
XLA Ops:
  0.7 1.2 copy.35
  2.0 1.0 fusion.1
  3.0 1.0 maximum_maximum_fusion.own_ref
  4.0 0.1 maximum_bitcast_fusion.1
  4.2 0.6 stack.26
  4.9 0.1 reshape.53
  5.0 0.8 pad.8.cotangent_ref
  5.7 0.1 reshape.52
  5.8 0.8 pad.7.tokens_ref
  6.6 176.4 %forward.1 = (bf16[6,4,4,4,256,256]{5,4,3,2,1,0:T(8,128)(2,1)}, f32[1,4,4,4,16,256]{5,4,3,2,1,0:T(8,128)}, bf16[4,208,256]{2,1,0:T(8,128)(2,1)}, bf16[4,208,256]...) custom-call(bf16[6,256,256]{2,1,0:T(8,128)(2,1)} %maximum_maximum_fu, ...), custom_call_target="tpu_custom_call" | custom-call | tf_op jit(solution)/shard_map/forward/pallas_call | solution.py:784
  183.0 193.5 %backward.1 = (bf16[4,208,256]{2,1,0:T(8,128)(2,1)}, bf16[4,208,256]{2,1,0:T(8,128)(2,1)}, f32[6,256,256]{2,1,0:T(8,128)}, f32[32,1024]{1,0:T(8,128)}) custom-call(bf16[6,4,4,4,256,256]{5,4,3,2,1,0:T(8,128)(2,1)} %get-tuple-element.28.full, f32[1,4,4,4,16,256]{5,4,3,2,1,0:T(8,128)} %get-tuple-element.29.small, ...), custom_call_target="tpu_custom_call" | custom-call | tf_op jit(solution)/shard_map/backward/pallas_call | solution.py:975
  376.5 1.3 fusion
  377.8 0.8 pad_maximum_fusion
  378.7 1.0 copy.43
  379.7 0.1 reshape.56
  379.8 0.6 pad_maximum_fusion.3
  380.5 0.6 slice_bitcast_fusion.1
  381.1 0.6 copy.42
  381.7 0.6 copy.41
  382.4 0.9 reshape.58
  383.3 0.9 reshape.59
  384.2 1.8 slice_bitcast_fusion
  386.0 0.6 copy.54
  386.6 1.6 slice.111
  (50 shorter events, 0.4 us)
Async XLA Ops:
  0.6 2.3 copy-start.4
  0.7 2.3 copy-start.6
  0.7 3.3 copy-start.7
  0.7 3.5 copy-start.10
  0.7 3.5 copy-start.11
  0.7 3.5 copy-start.12
  0.7 3.5 copy-start.8
  0.7 3.5 copy-start.9
  0.7 4.1 %copy-start = (f32[591,256]{1,0:T(8,128)S(1)}, f32[591,256]{1,0:T(8,128)}, u32[]{:S(2)}) copy-start(f32[591,256]{1,0:T(8,128)} %param.23) | copy-start | bytes 1815556
  3.0 2.7 copy-start.1
  377.8 1.9 copy-start.5
  378.6 3.7 copy-start.3
  379.7 3.6 copy-start.2

commit v3 on v2

--- a/solution.py
+++ b/solution.py
@@ -212,19 +212,15 @@
 
 
 def blockwise(shape, body):
-    lead = shape[:-2]
-    if not lead:
+    if len(shape) < 4:
         body(())
         return
 
     def step(i, _):
-        body((i // lead[1], i % lead[1]) if len(lead) == 2 else (i,))
+        body((i,))
         return 0
 
-    total = 1
-    for size in lead:
-        total *= size
-    lax.fori_loop(0, total, step, 0)
+    lax.fori_loop(0, shape[0], step, 0)
 
 
 def add_to(dst, first, *others):
@@ -325,11 +321,9 @@
         self.stay(step).start()
         self.go(step).start()
 
-    def handed(self):
+    def free_last(self):
         for step in (STEPS - 2, STEPS - 1):
             self.free(step)
-        for step in range(STEPS):
-            self.go(step).wait_recv()
 
     def join(self, *which):
         for by in which:
@@ -349,7 +343,8 @@
         return pltpu.make_async_copy(self.out, self.result, self.local)
 
     def open(self):
-        self.handed()
+        for step in range(STEPS):
+            self.go(step).wait_recv()
         self.join(2)
         self.each("opposite", self.one)
         self.join(1, -1)
@@ -381,15 +376,19 @@
         self.each("finish", self.two)
         self.each("finish", self.three)
 
-    def finish(self):
+    def shown(self):
         self.show().wait()
         self.keep().start()
-        self.keep().wait()
 
 
 def first_buffers():
     blocks = (RING,) * 3 + (CORE, 256)
-    return [pltpu.VMEM(blocks, BF16), pltpu.VMEM(blocks, BF16), pltpu.VMEM(blocks[1:], BF16), pltpu.VMEM((2,) + blocks[1:], BF16)]
+    return [pltpu.VMEM(blocks, BF16), pltpu.VMEM(blocks, BF16)]
+
+
+def pair_buffers():
+    blocks = (RING,) * 2 + (CORE, 256)
+    return [pltpu.VMEM(blocks, BF16), pltpu.VMEM((2,) + blocks, BF16)]
 
 
 def later_buffers():
@@ -636,6 +635,7 @@
 ]
 TOKENS = jax.ShapeDtypeStruct((ROWS, WIDTH), F32)
 TURNED = jax.ShapeDtypeStruct((RING, ROWS, 256), BF16)
+LOWS = jax.ShapeDtypeStruct((2, 2, ROWS, WIDTH), BF16)
 WEIGHTS = jax.ShapeDtypeStruct((6, RING, RING, RING, UNIT, 256), BF16)
 SMALLS = jax.ShapeDtypeStruct((1, RING, RING, RING, SMALL, 256), F32)
 
@@ -644,9 +644,9 @@
     return pltpu.VMEM(shape.shape, shape.dtype)
 
 
-def forward_kernel(own_ref, small_ref, tokens_ref, cotangent_ref, full, small_out, x0_out, g_out, mid_out, x1_out, end_out,
+def forward_kernel(own_ref, small_ref, tokens_ref, cotangent_ref, full, small_out, x0_out, g_out, mid_out, x1_out, end_out, low_out,
                    mixed_out, att_out, probs_out, act_out, slope_out,
-                   small, x0, resid, low, acc, mids, ends, slots, mixed_all, att_all, probs_all, act_all, slope_all, *sems):
+                   small, x0, resid, lows, acc, mids, ends, slots, mixed_all, att_all, probs_all, act_all, slope_all, *sems):
     place = Place()
     turn_x, turn_g = Turn(place, tokens_ref, x0, *sems[0:3]), Turn(place, cotangent_ref, g_out, *sems[3:6])
     load, saves, misc = sems[6:9]
@@ -666,24 +666,31 @@
     for copy in own_copies:
         copy.wait()
     gather.small_phase(1, "first")
-    gather.first_two(units[0])
-    gather.second_two(units[0])
+    for unit in units[:2]:
+        gather.first_two(unit)
+    for unit in units[:2]:
+        gather.second_two(unit)
     gather.small_phase(1, "second")
-    gather.first_two(units[1])
-    gather.third_two(units[0])
-    gather.first_three(units[0])
+    for unit in units[:2]:
+        gather.third_two(unit)
+        gather.first_three(unit)
+    for unit in units[2:]:
+        gather.first_two(unit)
     gather.small_phase(1, "third")
     gather.small_phase(2, "first")
-    gather.second_two(units[1])
-    gather.first_two(units[2])
-    gather.third_two(units[1])
+    gather.second_three(units[0])
+    for unit in units[2:]:
+        gather.second_two(unit)
     gather.small_phase(2, "second")
-    gather.second_three(units[0])
-    gather.first_three(units[1])
-    gather.small_phase(2, "third")
+    gather.second_three(units[1])
     turn_x.end()
     resid[...] = as_rows(x0)
     gather.third_three(units[0])
+    for unit in units[2:]:
+        gather.third_two(unit)
+    for unit in units[2:4]:
+        gather.first_three(unit)
+    gather.small_phase(2, "third")
     gather.ready(units[0])
     kept = []
 
@@ -698,23 +705,22 @@
 
     for k, (kind, layer) in enumerate(ORDER):
         unit = units[k]
-        hooks = {0: [], 1: [], 3: []}
-        if k + 2 < 6:
-            hooks[0] += [functools.partial(gather.second_two, units[k + 2])]
-            if k + 3 < 6:
-                hooks[0] += [functools.partial(gather.first_two, units[k + 3])]
-            hooks[0] += [functools.partial(gather.third_two, units[k + 2])]
+        hooks = {3: []}
         if k + 1 < 6:
-            hooks[1] += [functools.partial(gather.second_three, units[k + 1])]
+            hooks[3] += [functools.partial(gather.third_three, units[k + 1])]
             if k + 2 < 6:
-                hooks[1] += [functools.partial(gather.first_three, units[k + 2])]
-            hooks[3] += [functools.partial(gather.third_three, units[k + 1]), functools.partial(gather.ready, units[k + 1])]
+                hooks[3] += [functools.partial(gather.second_three, units[k + 2])]
+            if k + 4 < 6:
+                hooks[3] += [functools.partial(gather.first_three, units[k + 4])]
+            hooks[3] += [functools.partial(gather.ready, units[k + 1])]
 
         def save(which, src, dst, step):
             return pltpu.make_async_copy(src, dst, saves.at[which, k, step])
 
         if kind == 0:
+            low = lows.at[layer, 0]
             low[...] = norm_low(resid[...], small, layer, 0)
+            keep(low, low_out.at[layer, 0], 8 + 2 * layer)
             acc[...] = resid[...] + feature_row(small, layer, 4)
 
             def body(step, slot):
@@ -742,7 +748,9 @@
             if half == 0:
                 mids[layer] = acc[...]
                 resid[...] = acc[...]
+                low = lows.at[layer, 1]
                 low[...] = norm_low(resid[...], small, layer, 1)
+                keep(low, low_out.at[layer, 1], 9 + 2 * layer)
                 acc[...] = resid[...] + feature_row(small, layer, 5)
                 keep(mids.at[layer], mid_out.at[layer], 4 + layer)
 
@@ -783,14 +791,14 @@
     both = jax.ShapeDtypeStruct((2, ROWS, WIDTH), F32)
     return pl.pallas_call(
         forward_kernel,
-        out_shape=[WEIGHTS, SMALLS, TURNED, TURNED, both, TOKENS, TURNED, *SAVED],
+        out_shape=[WEIGHTS, SMALLS, TURNED, TURNED, both, TOKENS, TURNED, LOWS, *SAVED],
         in_specs=[VMEM] * 4,
-        out_specs=[ANY] * 12,
+        out_specs=[ANY] * 13,
         scratch_shapes=[
-            scratch_like(SMALLS), scratch_like(TURNED), scratch_like(TOKENS), pltpu.VMEM((ROWS, WIDTH), BF16),
+            scratch_like(SMALLS), scratch_like(TURNED), scratch_like(TOKENS), scratch_like(LOWS),
             scratch_like(TOKENS), scratch_like(both), scratch_like(TURNED), pltpu.VMEM((2, RING, RING, UNIT, 256), BF16),
             *[scratch_like(s) for s in SAVED],
-            *TURN_SEMAPHORES, *TURN_SEMAPHORES, DMA((6, 2, 1)), DMA((3, 6, STEPS)), DMA((8,)),
+            *TURN_SEMAPHORES, *TURN_SEMAPHORES, DMA((6, 2, 1)), DMA((3, 6, STEPS)), DMA((12,)),
             *gather_semaphores(),
         ],
         compiler_params=pltpu.CompilerParams(vmem_limit_bytes=VMEM_LIMIT, collective_id=0, has_side_effects=True),
@@ -801,27 +809,43 @@
 BACK = [(2, 1), (1, 1), (0, 1), (2, 0), (1, 0), (0, 0)]
 
 
-def backward_kernel(full, small, x0_ref, g_ref, mid_ref, x1_ref, end_ref, mixed_in, att_in, probs_in, act_in, slope_in,
+def backward_kernel(full, small_in, x0_in, g_in, mid_in, x1_in, end_ref, lows_in, mixed_in, att_in, probs_in, act_in, slope_in,
                     encoded_out, tokens_out, grads_out, sums_out,
-                    grad, low, here, acc, turned, sums, columns_all, slots, mixed_two, att_two, probs_two, act_two, slope_two, stage, outs,
+                    grad, low, acc, turned, small, lows, xbuf, sums, columns_all, slots, mixed_two, att_two, probs_two, act_two, slope_two, stage, outs,
                     *rest):
-    first = [rest[0:4], rest[4:8]]
-    later = [rest[8:14], rest[14:20]]
-    total_scratch, sems = rest[20:26], rest[26:]
+    first, pair = [rest[0:2], rest[2:4], rest[4:6]], [rest[6:8], rest[8:10]]
+    later = [rest[10:16], rest[16:22]]
+    total_scratch, sems = rest[22:28], rest[28:]
     place = Place()
     turn_out, turn_g = Turn(place, end_ref, encoded_out, *sems[0:3]), Turn(place, turned, tokens_out, *sems[3:6])
-    load, free = sems[6:8]
-    unit_sems = [[group.at[k] for group in sems[8:]] for k in range(6)]
+    load, free, misc = sems[6:9]
+    unit_sems = [[group.at[k] for group in sems[9:]] for k in range(6)]
     scatters = []
     for k, (kind, layer) in enumerate(BACK):
         scatters.append(
-            Scatter(place, kind, layer, stage, first[k % 2], later[k % 2][0:3], later[k % 2][3:6], outs.at[k],
+            Scatter(place, kind, layer, stage, [*first[k % 3], *pair[k % 2]], later[k % 2][0:3], later[k % 2][3:6], outs.at[k],
                     grads_out.at[number(kind, layer)], unit_sems[k])
         )
     total = Total(place, sums, total_scratch[0], sums_out, *total_scratch[1:])
+    norms = [(1, 1), (1, 0), (0, 1), (0, 0)]
+
+    def fetch_low(phase):
+        return pltpu.make_async_copy(lows_in.at[norms[phase][0], norms[phase][1]], lows.at[phase % 2], misc.at[phase])
+
+    def fetch_x(phase):
+        source = (mid_in.at[1], x1_in, mid_in.at[0], x0_in)[phase]
+        return pltpu.make_async_copy(source, turned if phase == 3 else xbuf, misc.at[4 + phase])
+
+    starts = [pltpu.make_async_copy(g_in, turned, misc.at[8]),
+              pltpu.make_async_copy(small_in.at[:, pl.ds(0, 1), pl.ds(0, 1)], small, misc.at[9]),
+              fetch_low(0)]
+    for copy in starts:
+        copy.start()
     place.greet(TOTAL_PEERS)
     turn_out.start()
-    grad[...] = as_rows(g_ref)
+    for copy in starts:
+        copy.wait()
+    grad[...] = as_rows(turned)
     sums[...] = jnp.zeros_like(sums)
     columns_all[...] = jnp.zeros_like(columns_all)
 
@@ -834,13 +858,18 @@
     for k, (kind, layer) in enumerate(BACK):
         it = scatters[k]
         hooks = {0: [], 1: [], 2: [], 3: []}
+        if k >= 1:
+            hooks[0] += [scatters[k - 1].open]
+            hooks[2] += [scatters[k - 1].sides_one]
         if k >= 2:
-            hooks[0] += [scatters[k - 2].sides_two]
-        if k >= 1:
-            hooks[1] += [scatters[k - 1].sides_one]
+            hooks[1] += [scatters[k - 2].centre_one, scatters[k - 2].start_two]
+            hooks[2] += [scatters[k - 2].sides_two]
+            hooks[3] += [scatters[k - 2].centre_two]
+        if k >= 3:
+            hooks[0] += [scatters[k - 3].sides_three]
+            hooks[1] += [scatters[k - 3].centre_three]
         if k >= 2:
-            hooks[1] += [scatters[k - 2].centre_two]
-            hooks[2] += [scatters[k - 2].sides_three]
+            hooks[1] += [functools.partial(leave, k + 1)]
         base = LAYER_SUMS * layer
 
         def begin(step):
@@ -848,14 +877,20 @@
             def _():
                 it.free(step - 2)
 
-            if k >= 2:
+            if k >= 1:
                 @pl.when(step == 0)
                 def _():
-                    may(k)
+                    scatters[k - 1].free_last()
+                    if k >= 3:
+                        may(k)
 
         if kind == 0:
-            x = as_rows(x0_ref) if layer == 0 else x1_ref[...]
-            here[...] = norm_low(x, small, layer, 0)
+            phase = 3 - 2 * layer
+            here = lows.at[phase % 2]
+            fetch_low(phase).wait()
+            if phase < 3:
+                fetch_low(phase + 1).start()
+            fetch_x(phase).start()
             low[...] = grad[...].astype(BF16)
             acc[...] = jnp.zeros_like(acc)
 
@@ -891,8 +926,13 @@
             ]
         else:
             half = kind - 1
+            phase = 2 - 2 * layer
+            here = lows.at[phase % 2]
             if half == 1:
-                here[...] = norm_low(mid_ref[layer], small, layer, 1)
+                if phase > 0:
+                    fetch_low(phase).wait()
+                fetch_low(phase + 1).start()
+                fetch_x(phase).start()
                 low[...] = grad[...].astype(BF16)
                 acc[...] = jnp.zeros_like(acc)
 
@@ -918,7 +958,8 @@
         Stream(pairs, load.at[k]).run(body, hooks)
         if kind < 2:
             j = kind
-            x = mid_ref[layer] if kind == 1 else (as_rows(x0_ref) if layer == 0 else x1_ref[...])
+            fetch_x(phase).wait()
+            x = as_rows(turned) if phase == 3 else xbuf[...]
             part, gain, shift = norm_back(acc[...], x, feature_row(small, layer, j))
             at = base + (8 if kind == 1 else 11)
             sums[at : at + 1, :] = jnp.sum(low[...].astype(F32), axis=0, keepdims=True)
@@ -934,63 +975,65 @@
                         at = LAYER_SUMS * i + STEPS * which + step
                         sums[at : at + 1, :] = columns_all[i, which, step]
             total.start()
-        it.open()
-        if k >= 1:
-            scatters[k - 1].centre_one()
-        if k >= 2:
-            scatters[k - 2].centre_three()
-        if 1 <= k <= 5:
-            leave(k + 1)
-        if k >= 1:
-            scatters[k - 1].start_two()
     early, late = scatters[4], scatters[5]
+    late.free_last()
+    may(6)
+    late.open()
+    scatters[3].sides_three()
     total.core_sum()
+    early.centre_one()
+    early.start_two()
+    scatters[3].centre_three()
+    leave(7)
+    late.sides_one()
+    total.put(1, total.take(0))
     early.sides_two()
-    late.sides_one()
     early.centre_two()
-    total.put(1, total.take(0))
+    for it in scatters[:4]:
+        it.shown()
+    total.put(2, total.take(1))
+    early.sides_three()
     late.centre_one()
-    may(6)
+    may(7)
     late.start_two()
-    early.sides_three()
-    total.put(2, total.take(1))
-    late.sides_two()
     early.centre_three()
     total.last()
+    late.sides_two()
     late.centre_two()
-    late.sides_three()
-    for it in scatters[:4]:
-        it.finish()
-    late.centre_three()
     turn_out.end()
     turn_g.end()
+    late.sides_three()
+    early.shown()
     total.finish()
-    early.finish()
-    late.finish()
-
-
-def backward(full, small, x0, g, mids, x1, ends, saved):
+    late.centre_three()
+    late.shown()
+    for it in scatters:
+        it.keep().wait()
+
+
+def backward(full, small, x0, g, mids, x1, ends, lows, saved):
     saved_two = [pltpu.VMEM((2,) + s.shape[-3 if len(s.shape) == 5 and s.shape[1] == STEPS else -2 :], s.dtype) for s in SAVED]
     semaphores = [pltpu.SemaphoreType.DMA((6,) + (s.shape if hasattr(s, "shape") else ())) for s in scatter_semaphores()]
     return pl.pallas_call(
         backward_kernel,
         out_shape=[TURNED, TURNED, jax.ShapeDtypeStruct((6, UNIT, 256), F32), jax.ShapeDtypeStruct((SUM_ROWS, WIDTH), F32)],
-        in_specs=[ANY] + [VMEM] * 6 + [ANY] * 5,
+        in_specs=[ANY] * 13,
         out_specs=[ANY] * 4,
         scratch_shapes=[
-            scratch_like(TOKENS), pltpu.VMEM((ROWS, WIDTH), BF16), pltpu.VMEM((ROWS, WIDTH), BF16), scratch_like(TOKENS),
-            scratch_like(TURNED), pltpu.VMEM((SUM_ROWS, WIDTH), F32), pltpu.VMEM((2, 2, STEPS, 1, WIDTH), F32),
+            scratch_like(TOKENS), pltpu.VMEM((ROWS, WIDTH), BF16), scratch_like(TOKENS),
+            scratch_like(TURNED), pltpu.VMEM((1, 1, 1, RING, SMALL, 256), F32), pltpu.VMEM((2, ROWS, WIDTH), BF16), scratch_like(TOKENS),
+            pltpu.VMEM((SUM_ROWS, WIDTH), F32), pltpu.VMEM((2, 2, STEPS, 1, WIDTH), F32),
             pltpu.VMEM((2, RING, RING, UNIT, 256), BF16),
             *saved_two,
             pltpu.VMEM((2, RING, RING, UNIT, 256), BF16), pltpu.VMEM((6, UNIT, 256), F32),
-            *first_buffers(), *first_buffers(), *later_buffers(), *later_buffers(),
+            *first_buffers(), *first_buffers(), *first_buffers(), *pair_buffers(), *pair_buffers(), *later_buffers(), *later_buffers(),
             *total_buffers(SUM_ROWS),
-            *TURN_SEMAPHORES, *TURN_SEMAPHORES, DMA((6, 2, 4)), pltpu.SemaphoreType.REGULAR((7,)),
+            *TURN_SEMAPHORES, *TURN_SEMAPHORES, DMA((6, 2, 4)), pltpu.SemaphoreType.REGULAR((8,)), DMA((10,)),
             *semaphores,
         ],
         compiler_params=pltpu.CompilerParams(vmem_limit_bytes=VMEM_LIMIT, collective_id=1, has_side_effects=True),
         name="backward",
-    )(full, small, x0, g, mids, x1, ends, *saved)
+    )(full, small, x0, g, mids, x1, ends, lows, *saved)
 
 
 def to_images(rows):
@@ -1010,10 +1053,10 @@
     zeros = jnp.zeros((layers, HEAD), F32)
     qkv_row = jnp.concatenate([qv_bias[:, :HEAD], zeros, qv_bias[:, HEAD:], zeros], axis=1)
     small = jnp.stack([norm_gain[:, 0], norm_gain[:, 1], norm_shift[:, 0], norm_shift[:, 1], proj_bias, down_bias, up_bias, qkv_row], axis=1)
-    full, small, x0, g, mids, x1, ends, *saved = forward(
+    full, small, x0, g, mids, x1, ends, lows, *saved = forward(
         own, small.reshape(1, SMALL, 256), to_images(tokens), to_images(cotangent.astype(BF16))
     )
-    encoded, grad_tokens, grads, sums = backward(full, small, x0, g, mids, x1, ends, saved)
+    encoded, grad_tokens, grads, sums = backward(full, small, x0, g, mids, x1, ends, lows, saved)
     row, col = lax.axis_index("row"), lax.axis_index("col")
     sums = sums[: layers * LAYER_SUMS].reshape(layers, LAYER_SUMS, WIDTH)
     up_sums = lax.dynamic_slice_in_dim(sums[:, 0:4].reshape(layers, 16, 256), col, 1, 1)[:, 0]

time: 389 us -> 342 us (0.88)
  Pallas kernels: 370 us -> 323 us
    pallas_call x1, Pallas kernels: 176 us -> 150 us  [forward(): pl.pallas_call(forward_kernel, out_shape=[WEIGHTS, SMALLS, TURNED, TURNED...]
    pallas_call x1, Pallas kernels: 194 us -> 173 us  [backward(): pl.pallas_call(backward_kernel, out_shape=[TURNED, TURNED, jax.ShapeDtype...]
where the time goes in v3:
time: 342 us; the launch traced here: 341 us
  Pallas kernels  323 us (94%)
  local copies, waits for them, and re-layouts  14.7 us (4%)
    pallas_call x1, Pallas kernels, backward(): pl.pallas_call(backward_kernel, out_shape=[TURNED, TURNED, jax.ShapeDtype...  173 us
    pallas_call x1, Pallas kernels, forward(): pl.pallas_call(forward_kernel, out_shape=[WEIGHTS, SMALLS, TURNED, TURNED...  150 us

profile of v3, /device:TPU:1, one launch (start us, length us, event | category | flops | bytes accessed | tf_op | source)
XLA Modules:
  0.0 340.8 jit_solution(10497427803298625086)
XLA Ops:
  0.7 1.2 copy.35
  2.0 1.0 fusion.1
  3.0 0.9 maximum_maximum_fusion.own_ref
  4.0 0.1 maximum_bitcast_fusion.1
  4.2 0.6 stack.26
  4.9 0.1 reshape.53
  5.0 0.8 pad.8.cotangent_ref
  5.7 0.1 reshape.52
  5.8 0.8 pad.7.tokens_ref
  6.6 149.8 %forward.1 = (bf16[6,4,4,4,256,256]{5,4,3,2,1,0:T(8,128)(2,1)}, f32[1,4,4,4,16,256]{5,4,3,2,1,0:T(8,128)}, bf16[4,208,256]{2,1,0:T(8,128)(2,1)}, bf16[4,208,256]...) custom-call(bf16[6,256,256]{2,1,0:T(8,128)(2,1)} %maximum_maximum_fu, ...), custom_call_target="tpu_custom_call" | custom-call | tf_op jit(solution)/shard_map/forward/pallas_call | solution.py:792
  156.4 172.8 %backward.1 = (bf16[4,208,256]{2,1,0:T(8,128)(2,1)}, bf16[4,208,256]{2,1,0:T(8,128)(2,1)}, f32[6,256,256]{2,1,0:T(8,128)}, f32[32,1024]{1,0:T(8,128)}) custom-call(bf16[6,4,4,4,256,256]{5,4,3,2,1,0:T(8,128)(2,1)} %get-tuple-element.29.full, f32[1,4,4,4,16,256]{5,4,3,2,1,0:T(8,128)} %get-tuple-element.30.small_in, ...), custom_call_target="tpu_custom_call" | custom-call | tf_op jit(solution)/shard_map/backward/pallas_call | solution.py:1017
  329.2 1.3 fusion
  330.5 0.8 pad_maximum_fusion
  331.3 1.0 copy.43
  332.4 0.1 reshape.56
  332.5 0.6 pad_maximum_fusion.3
  333.2 0.6 slice_bitcast_fusion.1
  333.8 0.6 copy.42
  334.4 0.6 copy.41
  335.1 0.9 reshape.58
  336.0 0.9 reshape.59
  336.9 1.8 slice_bitcast_fusion
  338.7 0.6 copy.54
  339.3 1.6 slice.111
  (50 shorter events, 0.4 us)
Async XLA Ops:
  0.6 2.3 copy-start.4
  0.7 2.3 copy-start.6
  0.7 3.3 copy-start.7
  0.7 3.5 %copy-start.10 = (f32[2,256]{1,0:T(2,128)S(1)}, f32[2,256]{1,0:T(2,128)}, u32[]{:S(2)}) copy-start(f32[2,256]{1,0:T(2,128)} %param.18) | copy-start | bytes 6148
  0.7 3.5 %copy-start.11 = (f32[2,256]{1,0:T(2,128)S(1)}, f32[2,256]{1,0:T(2,128)}, u32[]{:S(2)}) copy-start(f32[2,256]{1,0:T(2,128)} %param.22) | copy-start | bytes 6148
  0.7 3.5 %copy-start.12 = (f32[2,256]{1,0:T(2,128)S(1)}, f32[2,256]{1,0:T(2,128)}, u32[]{:S(2)}) copy-start(f32[2,256]{1,0:T(2,128)} %param.20) | copy-start | bytes 6148
  0.7 3.5 %copy-start.8 = (f32[2,2,256]{2,1,0:T(2,128)S(1)}, f32[2,2,256]{2,1,0:T(2,128)}, u32[]{:S(2)}) copy-start(f32[2,2,256]{2,1,0:T(2,128)} %param.13) | copy-start | bytes 12292
  0.7 3.5 %copy-start.9 = (f32[2,2,256]{2,1,0:T(2,128)S(1)}, f32[2,2,256]{2,1,0:T(2,128)}, u32[]{:S(2)}) copy-start(f32[2,2,256]{2,1,0:T(2,128)} %param.14) | copy-start | bytes 12292
  0.7 4.1 %copy-start = (f32[591,256]{1,0:T(8,128)S(1)}, f32[591,256]{1,0:T(8,128)}, u32[]{:S(2)}) copy-start(f32[591,256]{1,0:T(8,128)} %param.23) | copy-start | bytes 1815556
  3.0 2.7 copy-start.1
  330.5 1.9 copy-start.5
  331.3 3.7 %copy-start.3 = (bf16[4,208,256]{2,1,0:T(8,128)(2,1)S(1)}, bf16[4,208,256]{2,1,0:T(8,128)(2,1)}, u32[]{:S(2)}) copy-start(bf16[4,208,256]{2,1,0:T(8,128)(2,1)} %get-tuple-element.42) | copy-start | bytes 1277956
  332.3 3.6 %copy-start.2 = (bf16[4,208,256]{2,1,0:T(8,128)(2,1)S(1)}, bf16[4,208,256]{2,1,0:T(8,128)(2,1)}, u32[]{:S(2)}) copy-start(bf16[4,208,256]{2,1,0:T(8,128)(2,1)} %get-tuple-element.43) | copy-start | bytes 1277956

commit v4 on v3

--- a/solution.py
+++ b/solution.py
@@ -74,12 +74,12 @@
 
 
 class Ring:
-    def __init__(self, place, full, units, order, phase, start, count, half, send, recv, own=None):
+    def __init__(self, place, full, units, order, phase, start, count, half, sems, own=None):
         self.place, self.full, self.units, self.own = place, full, units, own
         self.axis, self.whole = order[phase], order[:phase]
         self.start, self.count = start, count
         self.halves = ((start, half), (start + half, count - half))
-        self.send, self.recv = send, recv
+        self.whole_send, self.half_send, self.whole_recv, self.half_recv = sems
 
     def piece(self, by, start, count):
         at = self.place.shifted(self.axis, by)
@@ -91,20 +91,20 @@
 
     def whole_copy(self, i):
         here = self.piece(0, self.start, self.count)
-        return remote(here if self.own is None else self.own, here, self.send.at[i], self.recv.at[i], self.to(i))
+        return remote(here if self.own is None else self.own, here, self.whole_send[i], self.whole_recv[i], self.to(i))
 
     def half_copy(self, i):
         ref = self.piece((-1, 1)[i], *self.halves[i])
-        return remote(ref, ref, self.send.at[2 + i], self.recv.at[2 + i], self.to(i))
-
-    def share(self, k):
-        ref = self.piece((-1, 1)[k], self.start, self.count) if k < 2 else self.piece(2, *self.halves[k - 2])
-        return remote(ref, ref, self.send.at[4 + k], self.recv.at[4 + k], self.place.sibling())
-
-    def share_all(self):
-        index = tuple(pl.ds(0, RING) if a in self.whole + (self.axis,) else self.place.at[a] for a in AXES)
-        ref = self.full.at[(self.units,) + index + (pl.ds(self.start, self.count),)]
-        return remote(ref, ref, self.send.at[4], self.recv.at[4], self.place.sibling())
+        return remote(ref, ref, self.half_send[i], self.half_recv[i], self.to(i))
+
+    def share(self, send, recv, *which):
+        for by in which:
+            if by is None:
+                index = tuple(pl.ds(0, RING) if a in self.whole + (self.axis,) else self.place.at[a] for a in AXES)
+                ref = self.full.at[(self.units,) + index + (pl.ds(self.start, self.count),)]
+            else:
+                ref = self.piece(by, self.start, self.count)
+            remote(ref, ref, send, recv, self.place.sibling()).start()
 
     def first(self):
         for i in range(2):
@@ -112,103 +112,141 @@
 
     def second(self):
         for i in range(2):
-            self.whole_copy(i).wait_recv()
             self.half_copy(i).start()
-
-    def third(self):
-        for i in range(2):
-            self.half_copy(i).wait_recv()
-
-    def finish(self):
-        for i in range(2):
-            self.whole_copy(i).wait_send()
-            self.half_copy(i).wait_send()
 
 
 class Gather:
     def __init__(self, place, own, full, small_own, small_full, sems):
-        one_send, one_recv, two_send, two_recv, three_send, three_recv, small_send, small_recv = sems
+        self.place, self.full = place, full
+        self.send, self.whole, self.half, self.share_send, self.share_recv, small_send, small_recv = sems
         self.one, self.two, self.three = [], {}, {}
         base = pl.multiple_of(place.core * CORE, CORE)
+
+        def shared(k):
+            return tuple([group.at[k]] * 2 for group in (self.send, self.send, self.whole, self.half))
+
         for kind in range(KINDS):
             for p, (start, count) in enumerate(CUTS[kind]):
                 rows = base + start
                 self.one.append(
-                    Ring(place, full, pl.ds(2 * kind, 2), ORDERS[p], 0, rows, count, 16, one_send.at[kind, p],
-                         one_recv.at[kind, p], own.at[pl.ds(2 * kind, 2), pl.ds(rows, count)])
+                    Ring(place, full, pl.ds(2 * kind, 2), ORDERS[p], 0, rows, count, 16, shared(0),
+                         own.at[pl.ds(2 * kind, 2), pl.ds(rows, count)])
                 )
             for layer in range(2):
                 u = number(kind, layer)
-                for phase, into, send, recv in ((1, self.two, two_send, two_recv), (2, self.three, three_send, three_recv)):
+                for phase, into in ((1, self.two), (2, self.three)):
                     into[u] = [
                         Ring(place, full, u, ORDERS[p], phase, base + start, count,
-                             count // 2 if count == 32 else (16, 32)[(p + layer) % 2], send.at[u, p], recv.at[u, p])
+                             count // 2 if count == 32 else (16, 32)[(p + layer) % 2], shared(self.place_of(u, phase)))
                         for p, (start, count) in enumerate(CUTS[kind])
                     ]
         rows = small_own.shape[1]
         self.small = [
-            Ring(place, small_full, pl.ds(0, 1), ORDERS[0], phase, 0, rows, rows // 2, small_send.at[phase],
-                 small_recv.at[phase], small_own if phase == 0 else None)
+            Ring(place, small_full, pl.ds(0, 1), ORDERS[0], phase, 0, rows, rows // 2,
+                 [[group.at[phase, k + i] for i in range(2)] for group, k in
+                  ((small_send, 0), (small_send, 2), (small_recv, 0), (small_recv, 2))],
+                 small_own if phase == 0 else None)
             for phase in range(3)
         ]
 
+    @staticmethod
+    def place_of(u, phase):
+        return 0 if phase == 0 else 1 + u + 6 * (phase - 1)
+
+    def amount(self, u, phase, times):
+        if phase == 0:
+            return self.full.at[:, 0, 0, pl.ds(0, times), self.place.mine]
+        if phase == 1:
+            return self.full.at[u, pl.ds(0, times), :, 0, self.place.mine]
+        return self.full.at[u, pl.ds(0, times), :, :, self.place.mine]
+
+    def came(self, u, phase, sems, times):
+        ref = self.amount(u, phase, times)
+        at = self.place_of(u, phase)
+        remote(ref, ref, self.send.at[at], sems.at[at], self.place.sibling()).wait_recv()
+
+    def sent(self, u, phase):
+        ref = self.amount(u, phase, 3)
+        at = self.place_of(u, phase)
+        remote(ref, ref, self.send.at[at], self.whole.at[at], self.place.sibling()).wait_send()
+
+    def rings(self, u, phase):
+        return self.one if phase == 0 else (self.two if phase == 1 else self.three)[u]
+
+    def first(self, u, phase):
+        for ring in self.rings(u, phase):
+            ring.first()
+
+    def second(self, u, phase):
+        self.came(u, phase, self.whole, 2)
+        for ring in self.rings(u, phase):
+            ring.second()
+
+    def third(self, u, phase):
+        self.came(u, phase, self.half, 1)
+
     def begin(self):
-        rings = self.one + [self.small[0]]
-        for name in ("first", "second", "third"):
-            for ring in rings:
-                getattr(ring, name)()
+        self.first(0, 0)
+        self.small_phase(0, "first")
+        self.second(0, 0)
+        self.small_phase(0, "second")
+        self.third(0, 0)
+        self.small_phase(0, "third")
 
     def small_phase(self, phase, name):
-        getattr(self.small[phase], name)()
+        ring = self.small[phase]
+        if name == "first":
+            ring.first()
+            return
+        for i in range(2):
+            if name == "second":
+                ring.whole_copy(i).wait_recv()
+                ring.half_copy(i).start()
+            else:
+                ring.half_copy(i).wait_recv()
 
     def first_two(self, u):
-        for ring in self.two[u]:
-            ring.first()
+        self.first(u, 1)
 
     def second_two(self, u):
-        for ring in self.two[u]:
-            ring.second()
+        self.second(u, 1)
 
     def third_two(self, u):
-        for ring in self.two[u]:
-            ring.third()
+        self.third(u, 1)
+
+    def share(self, u, phase, *which):
+        for ring in self.rings(u, phase):
+            ring.share(self.share_send.at[u], self.share_recv.at[u], *which)
 
     def first_three(self, u):
-        for ring in self.three[u]:
-            ring.first()
-        for ring in self.two[u]:
-            ring.share_all().start()
+        self.first(u, 2)
+        self.share(u, 1, None)
 
     def second_three(self, u):
-        for ring in self.three[u]:
-            ring.second()
-        for ring in self.three[u]:
-            for k in range(2):
-                ring.share(k).start()
+        self.second(u, 2)
+        self.share(u, 2, -1, 1)
 
     def third_three(self, u):
-        for ring in self.three[u]:
-            ring.third()
-            for k in range(2, 4):
-                ring.share(k).start()
+        self.third(u, 2)
+        self.share(u, 2, 2)
 
     def ready(self, u):
-        for ring in self.two[u]:
-            ring.share_all().wait()
-            ring.finish()
-        for ring in self.three[u]:
-            for k in range(4):
-                ring.share(k).wait()
-            ring.finish()
+        ref = self.full.at[u, :, :, :, self.place.mine]
+        remote(ref, ref, self.share_send.at[u], self.share_recv.at[u], self.place.sibling()).wait()
 
     def finish(self):
-        for ring in self.one + self.small:
-            ring.finish()
+        self.sent(0, 0)
+        for u in range(6):
+            self.sent(u, 1)
+            self.sent(u, 2)
+        for ring in self.small:
+            for i in range(2):
+                ring.whole_copy(i).wait_send()
+                ring.half_copy(i).wait_send()
 
 
 def gather_semaphores():
-    return [DMA((KINDS, 3, 4)), DMA((KINDS, 3, 4)), DMA((6, 3, 5)), DMA((6, 3, 5)), DMA((6, 3, 8)), DMA((6, 3, 8)),
-            DMA((3, 4)), DMA((3, 4))]
+    return [DMA((13,)), DMA((13,)), DMA((13,)), DMA((6,)), DMA((6,)), DMA((3, 4)), DMA((3, 4))]
 
 
 def blockwise(shape, body):
@@ -237,52 +275,53 @@
 
 
 class Fold:
-    def __init__(self, place, order, phase, work, half_in, full_in, dst, start, count, half, send, recv):
+    def __init__(self, place, order, phase, work, half_in, full_in, dst, start, count, half, sems):
         self.place, self.work, self.half_in, self.full_in, self.dst = place, work, half_in, full_in, dst
         self.axis, self.whole = order[2 - phase], order[: 2 - phase]
         self.axes = tuple(a for a in AXES if a not in order[3 - phase :])
         self.start, self.count = start, count
         self.halves = ((start, half), (start + half, count - half))
-        self.send, self.recv = send, recv
+        self.send, self.half_recv, self.whole_recv = sems
         self.lead = (slice(None),) * (2 - phase)
 
     def piece(self, by, start, count, ref=None):
         ref = self.work if ref is None else ref
         return region(ref, self.axes, self.place.shifted(self.axis, by), self.whole, start, count)
 
-    def half_copy(self, i):
-        src = self.piece(2, *self.halves[i])
-        dst = self.half_in.at[self.lead + (pl.ds(*self.halves[i]),)]
-        return remote(src, dst, self.send.at[i], self.recv.at[i], self.place.neighbour(self.axis, (1, -1)[i]))
+    def came(self, start, count):
+        return self.half_in.at[self.lead + (pl.ds(start, count),)]
 
     def arrived(self, i):
         return self.full_in.at[(i,) + self.lead + (pl.ds(self.start, self.count),)]
 
-    def whole_copy(self, i):
+    def opposite(self):
+        for i in range(2):
+            src, dst = self.piece(2, *self.halves[i]), self.came(*self.halves[i])
+            remote(src, dst, self.send, self.half_recv, self.place.neighbour(self.axis, (1, -1)[i])).start()
+
+    def side(self, i):
         by = (1, -1)[i]
         src = self.piece(by, self.start, self.count)
-        return remote(src, self.arrived(i), self.send.at[2 + i], self.recv.at[2 + i], self.place.neighbour(self.axis, by))
-
-    def opposite(self):
-        for i in range(2):
-            self.half_copy(i).start()
+        remote(src, self.arrived(i), self.send, self.whole_recv, self.place.neighbour(self.axis, by)).start()
 
     def sides(self):
         for i in range(2):
-            self.half_copy(i).wait_recv()
             ref = self.piece((1, -1)[i], *self.halves[i])
-            add_to(ref, ref, self.half_in.at[self.lead + (pl.ds(*self.halves[i]),)])
-            self.whole_copy(i).start()
+            add_to(ref, ref, self.came(*self.halves[i]))
+            self.side(i)
 
     def centre(self):
+        add_to(self.dst, self.piece(0, self.start, self.count), self.arrived(0), self.arrived(1))
+
+    def direct(self):
         for i in range(2):
-            self.whole_copy(i).wait_recv()
-        add_to(self.dst, self.piece(0, self.start, self.count), self.arrived(0), self.arrived(1))
-
-    def finish(self):
-        for i in range(2):
-            self.half_copy(i).wait_send()
-            self.whole_copy(i).wait_send()
+            self.side(i)
+        src = self.piece(2, self.start, self.count)
+        remote(src, self.came(self.start, self.count), self.send, self.half_recv, self.place.neighbour(self.axis, 2)).start()
+
+    def direct_centre(self):
+        add_to(self.dst, self.piece(0, self.start, self.count), self.arrived(0), self.arrived(1),
+               self.came(self.start, self.count))
 
 
 class Scatter:
@@ -290,19 +329,27 @@
         self.place, self.stage = place, stage
         self.work, self.twin, reduced, inner = first[0], first[1], second[0], third[0]
         self.out, self.result = out, result
-        (self.near, self.far_send, self.far_recv, send, recv, self.show_send, self.show_recv, self.local) = sems
+        (self.near, self.far_send, self.far_recv, self.send, self.half, self.whole, self.show_send, self.show_recv,
+         self.local) = sems
         base = pl.multiple_of(place.core * CORE, CORE)
-
-        def parts(phase, work, half_in, full_in, dst_of):
-            return [
-                Fold(place, ORDERS[p], phase, work, half_in, full_in, dst_of(start, count), start, count,
-                     count // 2 if count == 32 else (16, 32)[(p + layer) % 2], send.at[phase, p], recv.at[phase, p])
+        self.works = (self.work, reduced, inner)
+        self.half_in = (first[2], second[1], third[1])
+        self.full_in = (first[3], second[2], third[2])
+        targets = (
+            lambda start, count: reduced.at[:, :, pl.ds(start, count)],
+            lambda start, count: inner.at[:, pl.ds(start, count)],
+            lambda start, count: out.at[pl.ds(base + start, count)],
+        )
+        self.parts = [
+            [
+                Fold(place, ORDERS[p], phase, self.works[phase], self.half_in[phase], self.full_in[phase],
+                     targets[phase](start, count), start, count,
+                     count // 2 if count == 32 else (16, 32)[(p + layer) % 2],
+                     (self.send.at[phase], self.half.at[phase], self.whole.at[phase]))
                 for p, (start, count) in enumerate(CUTS[kind])
             ]
-
-        self.one = parts(0, self.work, first[2], first[3], lambda start, count: reduced.at[:, :, pl.ds(start, count)])
-        self.two = parts(1, reduced, second[1], second[2], lambda start, count: inner.at[:, pl.ds(start, count)])
-        self.three = parts(2, inner, third[1], third[2], lambda start, count: out.at[pl.ds(base + start, count)])
+            for phase in range(3)
+        ]
 
     def stay(self, step):
         slot = step % 2
@@ -311,7 +358,7 @@
     def go(self, step):
         slot = step % 2
         return remote(self.stage.at[slot, :, :, self.place.other], self.twin.at[step], self.far_send.at[slot],
-                      self.far_recv.at[step], self.place.sibling())
+                      self.far_recv, self.place.sibling())
 
     def free(self, step):
         self.stay(step).wait()
@@ -327,13 +374,20 @@
 
     def join(self, *which):
         for by in which:
-            for part in self.one:
+            for part in self.parts[0]:
                 ref = part.piece(by, part.start, part.count)
                 add_to(ref, ref, part.piece(by, part.start, part.count, self.twin))
 
-    def each(self, name, parts):
-        for part in parts:
+    def each(self, name, phase):
+        for part in self.parts[phase]:
             getattr(part, name)()
+
+    def came(self, refs, sems, phase):
+        remote(refs[phase], refs[phase], self.send.at[phase], sems.at[phase], self.place.sibling()).wait_recv()
+
+    def sent(self, phase):
+        ref = self.works[phase].at[pl.ds(0, 3)]
+        remote(ref, ref, self.send.at[phase], self.half.at[phase], self.place.sibling()).wait_send()
 
     def show(self):
         ref = self.out.at[self.place.mine]
@@ -342,39 +396,51 @@
     def keep(self):
         return pltpu.make_async_copy(self.out, self.result, self.local)
 
+    def sides(self, phase):
+        self.came(self.half_in, self.half, phase)
+        self.each("sides", phase)
+
+    def centre(self, phase):
+        self.came(self.full_in, self.whole, phase)
+        self.each("centre", phase)
+
+    def direct_centre(self, phase):
+        self.came(self.full_in, self.whole, phase)
+        self.came(self.half_in, self.half, phase)
+        self.each("direct_centre", phase)
+
     def open(self):
-        for step in range(STEPS):
-            self.go(step).wait_recv()
+        remote(self.twin, self.twin, self.far_send.at[0], self.far_recv, self.place.sibling()).wait_recv()
         self.join(2)
-        self.each("opposite", self.one)
+        self.each("opposite", 0)
         self.join(1, -1)
 
     def sides_one(self):
-        self.each("sides", self.one)
+        self.sides(0)
         self.join(0)
 
     def centre_one(self):
-        self.each("centre", self.one)
-        self.each("finish", self.one)
+        self.centre(0)
+        self.sent(0)
 
     def start_two(self):
-        self.each("opposite", self.two)
+        self.each("opposite", 1)
 
     def sides_two(self):
-        self.each("sides", self.two)
+        self.sides(1)
 
     def centre_two(self):
-        self.each("centre", self.two)
-        self.each("opposite", self.three)
+        self.centre(1)
+        self.each("opposite", 2)
 
     def sides_three(self):
-        self.each("sides", self.three)
+        self.sides(2)
 
     def centre_three(self):
-        self.each("centre", self.three)
+        self.centre(2)
         self.show().start()
-        self.each("finish", self.two)
-        self.each("finish", self.three)
+        self.sent(1)
+        self.sent(2)
 
     def shown(self):
         self.show().wait()
@@ -399,7 +465,7 @@
 
 
 def scatter_semaphores():
-    return [DMA((2,)), DMA((2,)), DMA((STEPS,)), DMA((3, 3, 4)), DMA((3, 3, 4)), DMA, DMA, DMA]
+    return [DMA((2,)), DMA((2,)), DMA, DMA((3,)), DMA((3,)), DMA((3,)), DMA, DMA, DMA]
 
 
 class Turn:
@@ -705,13 +771,13 @@
 
     for k, (kind, layer) in enumerate(ORDER):
         unit = units[k]
-        hooks = {3: []}
+        hooks = {2: [], 3: []}
         if k + 1 < 6:
-            hooks[3] += [functools.partial(gather.third_three, units[k + 1])]
+            hooks[2] += [functools.partial(gather.third_three, units[k + 1])]
             if k + 2 < 6:
-                hooks[3] += [functools.partial(gather.second_three, units[k + 2])]
+                hooks[2] += [functools.partial(gather.second_three, units[k + 2])]
             if k + 4 < 6:
-                hooks[3] += [functools.partial(gather.first_three, units[k + 4])]
+                hooks[2] += [functools.partial(gather.first_three, units[k + 4])]
             hooks[3] += [functools.partial(gather.ready, units[k + 1])]
 
         def save(which, src, dst, step):
@@ -849,11 +915,11 @@
     sums[...] = jnp.zeros_like(sums)
     columns_all[...] = jnp.zeros_like(columns_all)
 
-    def leave(k):
-        place.tell(free.at[k], NEAR)
-
-    def may(k):
-        pl.semaphore_wait(free.at[k], len(NEAR))
+    def leave(k, peers=NEAR):
+        place.tell(free.at[k], peers)
+
+    def may(k, peers=NEAR):
+        pl.semaphore_wait(free.at[k], len(peers))
 
     for k, (kind, layer) in enumerate(BACK):
         it = scatters[k]
@@ -984,7 +1050,7 @@
     early.centre_one()
     early.start_two()
     scatters[3].centre_three()
-    leave(7)
+    leave(7, TOTAL_PEERS)
     late.sides_one()
     total.put(1, total.take(0))
     early.sides_two()
@@ -994,18 +1060,20 @@
     total.put(2, total.take(1))
     early.sides_three()
     late.centre_one()
-    may(7)
-    late.start_two()
+    may(7, TOTAL_PEERS)
+    late.each("direct", 1)
     early.centre_three()
     total.last()
-    late.sides_two()
-    late.centre_two()
+    late.direct_centre(1)
+    late.each("direct", 2)
     turn_out.end()
     turn_g.end()
-    late.sides_three()
     early.shown()
     total.finish()
-    late.centre_three()
+    late.direct_centre(2)
+    late.show().start()
+    late.sent(1)
+    late.sent(2)
     late.shown()
     for it in scatters:
         it.keep().wait()

time: 342 us -> 329 us (0.962)
  Pallas kernels: 323 us -> 310 us
    pallas_call x1, Pallas kernels: 173 us -> 166 us  [backward(): pl.pallas_call(backward_kernel, out_shape=[TURNED, TURNED, jax.ShapeDtype...]
    pallas_call x1, Pallas kernels: 150 us -> 144 us  [forward(): pl.pallas_call(forward_kernel, out_shape=[WEIGHTS, SMALLS, TURNED, TURNED...]
where the time goes in v4:
time: 329 us; the launch traced here: 328 us
  Pallas kernels  310 us (94%)
  local copies, waits for them, and re-layouts  14.7 us (4%)
    pallas_call x1, Pallas kernels, backward(): pl.pallas_call(backward_kernel, out_shape=[TURNED, TURNED, jax.ShapeDtype...  166 us
    pallas_call x1, Pallas kernels, forward(): pl.pallas_call(forward_kernel, out_shape=[WEIGHTS, SMALLS, TURNED, TURNED...  144 us

profile of v4, /device:TPU:1, one launch (start us, length us, event | category | flops | bytes accessed | tf_op | source)
XLA Modules:
  0.0 328.5 jit_solution(6375409767215069959)
XLA Ops:
  0.7 1.2 copy.35
  2.0 1.0 fusion.1
  3.0 0.9 maximum_maximum_fusion.own_ref
  4.0 0.1 maximum_bitcast_fusion.1
  4.2 0.6 stack.26
  4.9 0.1 reshape.53
  5.0 0.8 pad.8.cotangent_ref
  5.7 0.1 reshape.52
  5.8 0.8 pad.7.tokens_ref
  6.6 144.1 %forward.1 = (bf16[6,4,4,4,256,256]{5,4,3,2,1,0:T(8,128)(2,1)}, f32[1,4,4,4,16,256]{5,4,3,2,1,0:T(8,128)}, bf16[4,208,256]{2,1,0:T(8,128)(2,1)}, bf16[4,208,256]...) custom-call(bf16[6,256,256]{2,1,0:T(8,128)(2,1)} %maximum_maximum_fu, ...), custom_call_target="tpu_custom_call" | custom-call | tf_op jit(solution)/shard_map/forward/pallas_call | solution.py:858
  150.7 166.1 %backward.1 = (bf16[4,208,256]{2,1,0:T(8,128)(2,1)}, bf16[4,208,256]{2,1,0:T(8,128)(2,1)}, f32[6,256,256]{2,1,0:T(8,128)}, f32[32,1024]{1,0:T(8,128)}) custom-call(bf16[6,4,4,4,256,256]{5,4,3,2,1,0:T(8,128)(2,1)} %get-tuple-element.29.full, f32[1,4,4,4,16,256]{5,4,3,2,1,0:T(8,128)} %get-tuple-element.30.small_in, ...), custom_call_target="tpu_custom_call" | custom-call | tf_op jit(solution)/shard_map/backward/pallas_call | solution.py:1085
  316.8 1.3 fusion
  318.1 0.8 pad_maximum_fusion
  319.0 1.0 copy.43
  320.0 0.1 reshape.56
  320.1 0.6 pad_maximum_fusion.3
  320.8 0.6 slice_bitcast_fusion.1
  321.4 0.6 copy.42
  322.0 0.6 copy.41
  322.7 0.9 reshape.58
  323.6 0.9 reshape.59
  324.5 1.8 slice_bitcast_fusion
  326.3 0.6 copy.54
  326.9 1.6 slice.111
  (50 shorter events, 0.4 us)
Async XLA Ops:
  0.6 2.3 copy-start.4
  0.7 2.3 copy-start.6
  0.7 3.3 %copy-start.7 = (f32[2,128]{1,0:T(2,128)S(1)}, f32[2,128]{1,0:T(2,128)}, u32[]{:S(2)}) copy-start(f32[2,128]{1,0:T(2,128)} %param.16) | copy-start | bytes 3076
  0.7 3.5 %copy-start.10 = (f32[2,256]{1,0:T(2,128)S(1)}, f32[2,256]{1,0:T(2,128)}, u32[]{:S(2)}) copy-start(f32[2,256]{1,0:T(2,128)} %param.18) | copy-start | bytes 6148
  0.7 3.5 %copy-start.11 = (f32[2,256]{1,0:T(2,128)S(1)}, f32[2,256]{1,0:T(2,128)}, u32[]{:S(2)}) copy-start(f32[2,256]{1,0:T(2,128)} %param.22) | copy-start | bytes 6148
  0.7 3.5 %copy-start.12 = (f32[2,256]{1,0:T(2,128)S(1)}, f32[2,256]{1,0:T(2,128)}, u32[]{:S(2)}) copy-start(f32[2,256]{1,0:T(2,128)} %param.20) | copy-start | bytes 6148
  0.7 3.5 %copy-start.8 = (f32[2,2,256]{2,1,0:T(2,128)S(1)}, f32[2,2,256]{2,1,0:T(2,128)}, u32[]{:S(2)}) copy-start(f32[2,2,256]{2,1,0:T(2,128)} %param.13) | copy-start | bytes 12292
  0.7 3.5 %copy-start.9 = (f32[2,2,256]{2,1,0:T(2,128)S(1)}, f32[2,2,256]{2,1,0:T(2,128)}, u32[]{:S(2)}) copy-start(f32[2,2,256]{2,1,0:T(2,128)} %param.14) | copy-start | bytes 12292
  0.7 4.1 %copy-start = (f32[591,256]{1,0:T(8,128)S(1)}, f32[591,256]{1,0:T(8,128)}, u32[]{:S(2)}) copy-start(f32[591,256]{1,0:T(8,128)} %param.23) | copy-start | bytes 1815556
  3.0 2.7 copy-start.1
  318.1 1.9 copy-start.5
  318.9 3.7 %copy-start.3 = (bf16[4,208,256]{2,1,0:T(8,128)(2,1)S(1)}, bf16[4,208,256]{2,1,0:T(8,128)(2,1)}, u32[]{:S(2)}) copy-start(bf16[4,208,256]{2,1,0:T(8,128)(2,1)} %get-tuple-element.42) | copy-start | bytes 1277956
  320.0 3.6 %copy-start.2 = (bf16[4,208,256]{2,1,0:T(8,128)(2,1)S(1)}, bf16[4,208,256]{2,1,0:T(8,128)(2,1)}, u32[]{:S(2)}) copy-start(bf16[4,208,256]{2,1,0:T(8,128)(2,1)} %get-tuple-element.43) | copy-start | bytes 1277956

commit v5 on v4

--- a/solution.py
+++ b/solution.py
@@ -1046,32 +1046,32 @@
     may(6)
     late.open()
     scatters[3].sides_three()
-    total.core_sum()
     early.centre_one()
     early.start_two()
     scatters[3].centre_three()
     leave(7, TOTAL_PEERS)
+    total.core_sum()
     late.sides_one()
+    early.sides_two()
     total.put(1, total.take(0))
-    early.sides_two()
     early.centre_two()
-    for it in scatters[:4]:
-        it.shown()
-    total.put(2, total.take(1))
-    early.sides_three()
     late.centre_one()
     may(7, TOTAL_PEERS)
     late.each("direct", 1)
+    total.put(2, total.take(1))
+    early.sides_three()
+    late.direct_centre(1)
+    late.each("direct", 2)
+    for it in scatters[:4]:
+        it.shown()
     early.centre_three()
     total.last()
-    late.direct_centre(1)
-    late.each("direct", 2)
+    late.direct_centre(2)
+    late.show().start()
     turn_out.end()
     turn_g.end()
     early.shown()
     total.finish()
-    late.direct_centre(2)
-    late.show().start()
     late.sent(1)
     late.sent(2)
     late.shown()

time: 329 us -> 326 us (level)
  no operation moved by 1% of the time
where the time goes in v5:
time: 326 us; the launch traced here: 325 us
  Pallas kernels  307 us (94%)
  local copies, waits for them, and re-layouts  14.7 us (5%)
    pallas_call x1, Pallas kernels, backward(): pl.pallas_call(backward_kernel, out_shape=[TURNED, TURNED, jax.ShapeDtype...  163 us
    pallas_call x1, Pallas kernels, forward(): pl.pallas_call(forward_kernel, out_shape=[WEIGHTS, SMALLS, TURNED, TURNED...  144 us

profile of v5, /device:TPU:1, one launch (start us, length us, event | category | flops | bytes accessed | tf_op | source)
XLA Modules:
  0.0 325.4 jit_solution(11888863558799456804)
XLA Ops:
  0.7 1.2 copy.35
  2.0 1.0 fusion.1
  3.0 0.9 maximum_maximum_fusion.own_ref
  4.0 0.1 maximum_bitcast_fusion.1
  4.2 0.6 stack.26
  4.9 0.1 reshape.53
  5.0 0.8 pad.8.cotangent_ref
  5.7 0.1 reshape.52
  5.8 0.8 pad.7.tokens_ref
  6.6 144.1 %forward.1 = (bf16[6,4,4,4,256,256]{5,4,3,2,1,0:T(8,128)(2,1)}, f32[1,4,4,4,16,256]{5,4,3,2,1,0:T(8,128)}, bf16[4,208,256]{2,1,0:T(8,128)(2,1)}, bf16[4,208,256]...) custom-call(bf16[6,256,256]{2,1,0:T(8,128)(2,1)} %maximum_maximum_fu, ...), custom_call_target="tpu_custom_call" | custom-call | tf_op jit(solution)/shard_map/forward/pallas_call | solution.py:858
  150.7 163.0 %backward.1 = (bf16[4,208,256]{2,1,0:T(8,128)(2,1)}, bf16[4,208,256]{2,1,0:T(8,128)(2,1)}, f32[6,256,256]{2,1,0:T(8,128)}, f32[32,1024]{1,0:T(8,128)}) custom-call(bf16[6,4,4,4,256,256]{5,4,3,2,1,0:T(8,128)(2,1)} %get-tuple-element.29.full, f32[1,4,4,4,16,256]{5,4,3,2,1,0:T(8,128)} %get-tuple-element.30.small_in, ...), custom_call_target="tpu_custom_call" | custom-call | tf_op jit(solution)/shard_map/backward/pallas_call | solution.py:1085
  313.8 1.3 fusion
  315.1 0.8 pad_maximum_fusion
  315.9 1.0 copy.43
  317.0 0.1 reshape.56
  317.1 0.6 pad_maximum_fusion.3
  317.8 0.6 slice_bitcast_fusion.1
  318.4 0.6 copy.42
  319.0 0.6 copy.41
  319.6 0.9 reshape.58
  320.6 0.9 reshape.59
  321.5 1.8 slice_bitcast_fusion
  323.3 0.6 copy.54
  323.9 1.6 slice.111
  (50 shorter events, 0.4 us)
Async XLA Ops:
  0.6 2.3 copy-start.4
  0.7 2.3 copy-start.6
  0.7 3.3 %copy-start.7 = (f32[2,128]{1,0:T(2,128)S(1)}, f32[2,128]{1,0:T(2,128)}, u32[]{:S(2)}) copy-start(f32[2,128]{1,0:T(2,128)} %param.16) | copy-start | bytes 3076
  0.7 3.5 %copy-start.10 = (f32[2,256]{1,0:T(2,128)S(1)}, f32[2,256]{1,0:T(2,128)}, u32[]{:S(2)}) copy-start(f32[2,256]{1,0:T(2,128)} %param.18) | copy-start | bytes 6148
  0.7 3.5 %copy-start.11 = (f32[2,256]{1,0:T(2,128)S(1)}, f32[2,256]{1,0:T(2,128)}, u32[]{:S(2)}) copy-start(f32[2,256]{1,0:T(2,128)} %param.22) | copy-start | bytes 6148
  0.7 3.5 %copy-start.12 = (f32[2,256]{1,0:T(2,128)S(1)}, f32[2,256]{1,0:T(2,128)}, u32[]{:S(2)}) copy-start(f32[2,256]{1,0:T(2,128)} %param.20) | copy-start | bytes 6148
  0.7 3.5 %copy-start.8 = (f32[2,2,256]{2,1,0:T(2,128)S(1)}, f32[2,2,256]{2,1,0:T(2,128)}, u32[]{:S(2)}) copy-start(f32[2,2,256]{2,1,0:T(2,128)} %param.13) | copy-start | bytes 12292
  0.7 3.5 %copy-start.9 = (f32[2,2,256]{2,1,0:T(2,128)S(1)}, f32[2,2,256]{2,1,0:T(2,128)}, u32[]{:S(2)}) copy-start(f32[2,2,256]{2,1,0:T(2,128)} %param.14) | copy-start | bytes 12292
  0.7 4.1 %copy-start = (f32[591,256]{1,0:T(8,128)S(1)}, f32[591,256]{1,0:T(8,128)}, u32[]{:S(2)}) copy-start(f32[591,256]{1,0:T(8,128)} %param.23) | copy-start | bytes 1815556
  3.0 2.7 copy-start.1
  315.0 1.9 copy-start.5
  315.9 3.7 %copy-start.3 = (bf16[4,208,256]{2,1,0:T(8,128)(2,1)S(1)}, bf16[4,208,256]{2,1,0:T(8,128)(2,1)}, u32[]{:S(2)}) copy-start(bf16[4,208,256]{2,1,0:T(8,128)(2,1)} %get-tuple-element.42) | copy-start | bytes 1277956
  316.9 3.6 %copy-start.2 = (bf16[4,208,256]{2,1,0:T(8,128)(2,1)S(1)}, bf16[4,208,256]{2,1,0:T(8,128)(2,1)}, u32[]{:S(2)}) copy-start(bf16[4,208,256]{2,1,0:T(8,128)(2,1)} %get-tuple-element.43) | copy-start | bytes 1277956
